TPU v7x, 512 devices: a whole 4x8x8 slice. The times are simulated.
512 devices in a mesh: ep: 32 (over z, x), etp: 16 (over y, core).
Axes of the slice: x: 4, y: 8, z: 8, core: 2. Of those that a mesh axis runs over, the one named last changes fastest.
Arguments:
- tokens: bfloat16 [8192, 2560], P('ep', 'etp'), may hold values from -6 to 6
- grad_out: bfloat16 [8192, 2560], P('ep', 'etp'), may hold values from -6 to 6
- expert_ids: int32 [8192, 1], P('ep'), may hold values from 0 to 31; in each aligned block of 256 rows (0 to 255, 256 to 511, ...) at most 12 rows name the same one
- router: bfloat16 [2560, 32], P('etp'), may hold values from -0.078125 to 0.078125
- gate_weight: bfloat16 [32, 2560, 4096], P('ep', None, 'etp'), may hold values from -0.125 to 0.125
- up_weight: bfloat16 [32, 2560, 4096], P('ep', None, 'etp'), may hold values from -0.125 to 0.125
- down_weight: bfloat16 [32, 4096, 2560], P('ep', 'etp'), may hold values from -0.09375 to 0.09375
Outputs:
- d_tokens: bfloat16 [8192, 2560], P('ep', 'etp')
Inputs may be any that keep to these rules, and one draw needn't show every extreme that they name: `expert_ids`: within the 256 tokens of one index of ep (aligned blocks of tokens), no expert is chosen by more than 12 tokens; every expert is chosen by some token.
All inputs are finite; a program needn't handle non-finite values.
Results may differ from a plain program's by a relative error of at most 0.012.
Values may be sent and summed in bfloat16 or wider, within the bound.
No kernel may reach another device: no remote copies, remote signals or barrier semaphores. Data moves between devices by JAX's collectives and lax.ppermute only.
A program may use at most 128 MiB of HBM per device.

v0:
```python
import jax
import jax.numpy as jnp
from jax import lax
from jax.sharding import PartitionSpec as P


def silu_parts(gate_pre):
    sigmoid = jax.nn.sigmoid(gate_pre)
    return (gate_pre * sigmoid, sigmoid * (1.0 + gate_pre * (1.0 - sigmoid)))


def contract_last(left, right):
    return lax.dot_general(
        left, right, (((1,), (1,)), ((), ())), preferred_element_type=jnp.float32
    )


def input_grad(gate_pre, up_pre, d_hidden, w_gate, w_up):
    activated, slope_term = silu_parts(gate_pre)
    d_gate = (d_hidden * up_pre * slope_term).astype(jnp.bfloat16)
    d_up = (d_hidden * activated).astype(jnp.bfloat16)
    return contract_last(d_gate, w_gate) + contract_last(d_up, w_up)


def pack_slots(values, slot_index, experts, capacity):
    empty_grid = jnp.zeros((experts * capacity, values.shape[1]), values.dtype)
    return empty_grid.at[slot_index].set(values).reshape(experts, capacity, values.shape[1])


def body(tokens, grad_out, expert_ids, router, gate_weight, up_weight, down_weight):
    experts = lax.axis_size("ep")
    tok_rows = tokens.shape[0]
    capacity = 3 * tok_rows // (2 * experts)
    local_width = tokens.shape[1]
    full_width = lax.axis_size("etp") * local_width
    w_gate = gate_weight[0]
    w_up = up_weight[0]
    w_down = down_weight[0]
    chosen = expert_ids[:, 0]
    picked = chosen[:, None] == jnp.arange(experts, dtype=jnp.int32)[None, :]
    logits = jnp.dot(tokens, router, preferred_element_type=jnp.float32)
    logit_part = jnp.sum(jnp.where(picked, logits, 0.0), axis=1)
    logit_sum = lax.psum(logit_part, "etp")
    scores = jax.nn.sigmoid(logit_sum)
    routed = (scores[:, None] * tokens.astype(jnp.float32)).astype(jnp.bfloat16)
    running = jnp.cumsum(picked.astype(jnp.int32), axis=0) - 1
    slot_rank = jnp.sum(jnp.where(picked, running, 0), axis=1)
    slot_index = chosen * capacity + slot_rank
    full_in, full_grad = (
        lax.all_gather(routed, "etp", axis=1, tiled=True),
        lax.all_gather(grad_out, "etp", axis=1, tiled=True),
    )
    send_in = pack_slots(full_in, slot_index, experts, capacity)
    send_grad = pack_slots(full_grad, slot_index, experts, capacity)
    recv_in = lax.all_to_all(send_in, "ep", split_axis=0, concat_axis=0, tiled=True)
    recv_grad = lax.all_to_all(send_grad, "ep", split_axis=0, concat_axis=0, tiled=True)
    grid_shape = recv_in.shape
    flat_count = grid_shape[0] * grid_shape[1]
    flat_in = recv_in.reshape(flat_count, full_width)
    flat_grad = recv_grad.reshape(flat_count, full_width)
    gate_pre = jnp.dot(flat_in, w_gate, preferred_element_type=jnp.float32)
    up_pre = jnp.dot(flat_in, w_up, preferred_element_type=jnp.float32)
    d_hidden = contract_last(flat_grad, w_down)
    partial_value = input_grad(gate_pre, up_pre, d_hidden, w_gate, w_up)
    partial_value = partial_value.reshape(grid_shape[0], grid_shape[1], full_width)
    returned = lax.all_to_all(partial_value, "ep", split_axis=0, concat_axis=0, tiled=True)
    unpacked = returned.reshape(experts * capacity, full_width)[slot_index]
    d_routed = lax.psum_scatter(unpacked, "etp", scatter_dimension=1, tiled=True).astype(
        jnp.bfloat16
    )
    d_score_part = jnp.sum(d_routed.astype(jnp.float32) * tokens.astype(jnp.float32), axis=1)
    d_score = lax.psum(d_score_part, "etp")
    d_logit = d_score * scores * (1.0 - scores)
    router_cols = contract_last(picked.astype(jnp.bfloat16), router)
    d_tokens = scores[:, None] * d_routed.astype(jnp.float32) + d_logit[:, None] * router_cols
    return d_tokens.astype(jnp.bfloat16)


def solution(mesh):
    placed = (
        P("ep", "etp"),
        P("ep", "etp"),
        P("ep", None),
        P("etp", None),
        P("ep", None, "etp"),
        P("ep", None, "etp"),
        P("ep", "etp", None),
    )
    return jax.shard_map(
        body, mesh=mesh, in_specs=placed, out_specs=P("ep", "etp"), check_vma=False
    )
```

profile of v0, /device:TPU:1, one launch (start us, length us, event | category | flops | bytes accessed | tf_op | source)
XLA Modules:
  0.0 481.8 jit_solution(17724541973685204360)
XLA Ops:
  7.7 29.8 %psum.14 = f32[256]{0:T(256)S(1)} all-reduce(f32[256]{0:T(256)S(1)} %fusion.22), channel_id=1, replica_groups=mesh['ep'=32,'etp'=16] {'etp'}, use_global_device_ids=true, to_apply=%region_1.2 | all-reduce | flops 256 | bytes 2048 | tf_op jit(solution)/shard_map/psum | solution.py:43
  42.0 38.1 %all-gather.5.cloned.1.call-done = bf16[256,2560]{0,1:T(8,128)(2,1)} async-done(((bf16[256,160]{0,1:T(8,128)(2,1)}), bf16[256,2560]{0,1:T(8,128)(2,1)}) %all-gather.5.cloned.1.call-update) | async-done | bytes 1310736 | tf_op jit(solution)/shard_map/all_gather | solution.py:50
  80.1 2.4 copy.12
  82.5 3.8 scatter_custom_fusion.1
  88.5 10.0 %all-to-all-start.1 = ((bf16[32,12,2560]{2,1,0:T(8,128)(2,1)}), bf16[32,12,2560]{2,1,0:T(8,128)(2,1)}, u32[]{:S(2)}, u32[]{:S(2)}) async-start(bf16[32,12,2560]{2,1,0:T(8,128)(2,1)} %reshape.42), calls=%async_computation.1 | async-start | bytes 5242880 | tf_op jit(solution)/shard_map/all_to_all | solution.py:55
  99.3 42.2 %all-gather.3.cloned.1.call-done = bf16[256,2560]{0,1:T(8,128)(2,1)} async-done(((bf16[256,160]{0,1:T(8,128)(2,1)}), bf16[256,2560]{0,1:T(8,128)(2,1)}) %all-gather.3.cloned.1.call-update) | async-done | bytes 1310736 | tf_op jit(solution)/shard_map/all_gather | solution.py:51
  143.9 3.8 scatter_custom_fusion
  149.9 8.0 %all-to-all-done.1 = bf16[32,12,2560]{2,1,0:T(8,128)(2,1)} async-done(((bf16[32,12,2560]{2,1,0:T(8,128)(2,1)}), bf16[32,12,2560]{2,1,0:T(8,128)(2,1)}, u32[]{:S(2)}, u32[]{:S(2)}) %all-to-all-start.1) | async-done | bytes 1966112 | tf_op jit(solution)/shard_map/all_to_all | solution.py:55
  158.0 7.9 %all-to-all-start = ((bf16[32,12,2560]{2,1,0:T(8,128)(2,1)}), bf16[32,12,2560]{2,1,0:T(8,128)(2,1)}, u32[]{:S(2)}, u32[]{:S(2)}) async-start(bf16[32,12,2560]{2,1,0:T(8,128)(2,1)} %reshape.40), calls=%async_computation | async-start | bytes 5242880 | tf_op jit(solution)/shard_map/all_to_all | solution.py:56
  165.8 2.7 reshape.43
  168.5 2.7 fusion.2
  171.2 53.9 %all-to-all-done = bf16[32,12,2560]{2,1,0:T(8,128)(2,1)} async-done(((bf16[32,12,2560]{2,1,0:T(8,128)(2,1)}), bf16[32,12,2560]{2,1,0:T(8,128)(2,1)}, u32[]{:S(2)}, u32[]{:S(2)}) %all-to-all-start) | async-done | bytes 1966112 | tf_op jit(solution)/shard_map/all_to_all | solution.py:56
  225.2 4.0 reshape.41
  229.2 3.3 fusion.7
  232.5 5.6 %fusion = f32[384,2560]{1,0:T(8,128)} fusion(bf16[1,2560,256]{2,1,0:T(8,128)(2,1)} %param.11, f32[384,256]{1,0:T(8,128)} %fusion.7, bf16[384,2560]{1,0:T(8,128)(2,1)S(1)} %reshape.43, bf16[1,2560,256]{2,1,0:T(8,128)(2,1)S(1)} %copy-done, f32[384,256]{1,0:T(8,128)} %fusion.2), kind=kOutput, calls=%fused_computation.4 | convolution fusion | flops 1007616000 | bytes 9306112 | tf_op jit(solution)/shard_map/dot_general | solution.py:13
  238.1 5.0 %convolution_add_fusion = f32[384,2560]{1,0:T(8,128)} fusion(f32[384,2560]{1,0:T(8,128)} %fusion, bf16[1,2560,256]{2,1,0:T(8,128)(2,1)S(1)} %copy-done, f32[384,256]{1,0:T(8,128)} %fusion.7, f32[384,256]{1,0:T(8,128)} %fusion.2), kind=kOutput, calls=%fused_computation.3 | convolution fusion | flops 504889344 | bytes 9961472 | tf_op jit(solution)/shard_map/dot_general | solution.py:13
  243.1 5.0 %reshape.44 = f32[32,12,2560]{2,1,0:T(8,128)} reshape(f32[384,2560]{1,0:T(8,128)} %convolution_add_fusion) | data formatting | bytes 7864320 | tf_op jit(solution)/shard_map/reshape | solution.py:65
  248.1 7.6 %all-to-all-start.2 = ((f32[32,12,2560]{2,1,0:T(8,128)}), f32[32,12,2560]{2,1,0:T(8,128)}, u32[]{:S(2)}, u32[]{:S(2)}) async-start(f32[32,12,2560]{2,1,0:T(8,128)} %reshape.44), calls=%async_computation.2 | async-start | bytes 10485760 | tf_op jit(solution)/shard_map/all_to_all | solution.py:66
  255.8 114.5 %all-to-all-done.2 = f32[32,12,2560]{2,1,0:T(8,128)} async-done(((f32[32,12,2560]{2,1,0:T(8,128)}), f32[32,12,2560]{2,1,0:T(8,128)}, u32[]{:S(2)}, u32[]{:S(2)}) %all-to-all-start.2) | async-done | bytes 3932192 | tf_op jit(solution)/shard_map/all_to_all | solution.py:66
  370.3 5.0 %reshape.45 = f32[384,2560]{1,0:T(8,128)} reshape(f32[32,12,2560]{2,1,0:T(8,128)} %all-to-all-done.2) | data formatting | bytes 7864320 | tf_op jit(solution)/shard_map/reshape | solution.py:67
  375.3 6.2 %gather_fusion = f32[256,2560]{1,0:T(8,128)} fusion(f32[384,2560]{1,0:T(8,128)} %reshape.45, s32[1024]{0:T(1024)S(1)} %pad_clamp_fusion), kind=kCustom, calls=%fused_computation | custom fusion | bytes 5243904 | tf_op jit(solution)/shard_map/gather | solution.py:67
  381.6 3.3 copy.13
  384.8 62.2 %reduce-scatter.2.cloned.1.call-done = f32[256,160]{0,1:T(8,128)} async-done(((f32[256,2560]{0,1:T(8,128)}), f32[256,160]{0,1:T(8,128)}) %reduce-scatter.2.cloned.1.call-update) | async-done | bytes 163856 | tf_op jit(solution)/shard_map/reduce_scatter | solution.py:68
  448.0 25.5 %psum.15 = f32[256]{0:T(256)S(1)} all-reduce(f32[256]{0:T(256)S(1)} %fusion.34), channel_id=1, replica_groups=mesh['ep'=32,'etp'=16] {'etp'}, use_global_device_ids=true, to_apply=%region_9.10 | all-reduce | flops 256 | bytes 2048 | tf_op jit(solution)/shard_map/psum | solution.py:72
  (31 shorter events, 16.0 us)
Async XLA Ops:
  6.5 226.0 %copy-start = (bf16[1,2560,256]{2,1,0:T(8,128)(2,1)S(1)}, bf16[1,2560,256]{2,1,0:T(8,128)(2,1)}, u32[]{:S(2)}) copy-start(bf16[1,2560,256]{2,1,0:T(8,128)(2,1)} %param.12) | copy-start | bytes 3932164
  6.5 73.5 %all-gather.5.cloned.1.call-start = ((), (), s32[]{:S(2)}) async-start(), calls=%async_computation.5 | async-start | bytes 1392640 | tf_op jit(solution)/shard_map/all_gather | solution.py:50
  88.5 69.4 %all-to-all-start.1 = ((bf16[32,12,2560]{2,1,0:T(8,128)(2,1)}), bf16[32,12,2560]{2,1,0:T(8,128)(2,1)}, u32[]{:S(2)}, u32[]{:S(2)}) async-start(bf16[32,12,2560]{2,1,0:T(8,128)(2,1)} %reshape.42), calls=%async_computation.1 | async-start | bytes 5242880 | tf_op jit(solution)/shard_map/all_to_all | solution.py:55
  98.5 42.9 %all-gather.3.cloned.1.call-start = ((), (), s32[]{:S(2)}) async-start(), calls=%async_computation.4 | async-start | bytes 1392640 | tf_op jit(solution)/shard_map/all_gather | solution.py:51
  158.0 67.2 %all-to-all-start = ((bf16[32,12,2560]{2,1,0:T(8,128)(2,1)}), bf16[32,12,2560]{2,1,0:T(8,128)(2,1)}, u32[]{:S(2)}, u32[]{:S(2)}) async-start(bf16[32,12,2560]{2,1,0:T(8,128)(2,1)} %reshape.40), calls=%async_computation | async-start | bytes 5242880 | tf_op jit(solution)/shard_map/all_to_all | solution.py:56
  248.1 122.2 %all-to-all-start.2 = ((f32[32,12,2560]{2,1,0:T(8,128)}), f32[32,12,2560]{2,1,0:T(8,128)}, u32[]{:S(2)}, u32[]{:S(2)}) async-start(f32[32,12,2560]{2,1,0:T(8,128)} %reshape.44), calls=%async_computation.2 | async-start | bytes 10485760 | tf_op jit(solution)/shard_map/all_to_all | solution.py:66
  255.7 191.3 %reduce-scatter.2.cloned.1.call-start = ((), (), s32[]{:S(2)}) async-start(), calls=%async_computation.6 | async-start | bytes 2785280 | tf_op jit(solution)/shard_map/reduce_scatter | solution.py:68
  384.8 62.2 %copy-start.1 = (bf16[256,160]{0,1:T(8,128)(2,1)S(1)}, bf16[256,160]{0,1:T(8,128)(2,1)}, u32[]{:S(2)}) copy-start(bf16[256,160]{0,1:T(8,128)(2,1)} %param.7) | copy-start | bytes 245764
  384.8 88.6 %copy-start.2 = (bf16[160,32]{0,1:T(8,128)(2,1)S(1)}, bf16[160,32]{0,1:T(8,128)(2,1)}, u32[]{:S(2)}) copy-start(bf16[160,32]{0,1:T(8,128)(2,1)} %param.10) | copy-start | bytes 30724
  384.8 88.6 %copy-start.3 = (s32[256,1]{0,1:T(1,128)S(1)}, s32[256,1]{0,1:T(1,128)}, u32[]{:S(2)}) copy-start(s32[256,1]{0,1:T(1,128)} %param.9) | copy-start | bytes 3076
Sparse Core Ops, SparseCore 0:
  39.2 40.8 all-gather.4
  101.5 39.9 all-gather.2
  385.0 62.0 reduce-scatter.1
where the time goes:
time: 483 us; the launch traced here: 482 us
  waiting for transfers between devices  320 us (66%)
  blocking collectives  55.2 us (11%)
  local copies, waits for them, and re-layouts  43.3 us (9%)
  starting transfers between devices  25.6 us (5%)
  matrix products  19.6 us (4%)
  between operations  13.2 us (3%)
  other arithmetic  5.29 us (1%)
    all_to_all x1, waiting for transfers between devices, body(): lax.all_to_all(partial_value, 'ep', split_axis=0, concat_axis=0, tiled=True)  114 us
    reduce_scatter x1, waiting for transfers between devices, body(): lax.psum_scatter(unpacked, 'etp', scatter_dimension=1, tiled=True)  62.2 us
    all_to_all x1, waiting for transfers between devices, body(): lax.all_to_all(send_grad, 'ep', split_axis=0, concat_axis=0, tiled=True)  53.9 us
    all_gather x1, waiting for transfers between devices, body(): lax.all_gather(grad_out, 'etp', axis=1, tiled=True)  42.2 us
    all_gather x1, waiting for transfers between devices, body(): lax.all_gather(routed, 'etp', axis=1, tiled=True)  38.1 us
    psum x1, blocking collectives, body(): logit_sum = lax.psum(logit_part, 'etp')  29.8 us
    psum x1, blocking collectives, body(): d_score = lax.psum(d_score_part, 'etp')  25.5 us
    dot_general x4, matrix products, contract_last(): lax.dot_general(left, right, (((1,), (1,)), ((), ())), preferred_element_...  15.7 us
  transfers between devices with their start and end apart: 6, of which 6 were waited for; matrix products, arithmetic and copies ran while one was open for 3% of the time, Pallas kernels for 0%

commit v1 on v0

v1 whole, which is shorter than its diff:
```python
import jax
import jax.numpy as jnp
from jax import lax
from jax.experimental import pallas as pl
from jax.experimental.pallas import tpu as pltpu
from jax.sharding import PartitionSpec as P

CAP = 12
ROWS = 16
EXPERTS = 32
TOK = 256
WID = 160
N_ETP = 16
D = WID * N_ETP
HID = 256
SLOTS = EXPERTS * CAP
HALF = SLOTS // 2
GRID = EXPERTS * ROWS
AG_ROWS = 2 * WID + 16
F32 = jnp.float32
BF = jnp.bfloat16


def iota(shape, dim):
    return lax.broadcasted_iota(jnp.int32, shape, dim)


def dot(left, right, dims):
    return lax.dot_general(left, right, ((dims[:1], dims[1:]), ((), ())), preferred_element_type=F32)


def slot_lanes():
    row = iota((GRID, 1), 0)
    src, rank = row // ROWS, row % ROWS
    half = src // (EXPERTS // 2)
    at = (src % (EXPERTS // 2)) * CAP + rank
    lane = jnp.where(at < 128, half * 128 + at, 256 + half * 64 + at - 128)
    lane = jnp.where(rank < CAP, lane, -1)
    return (lane == iota((GRID, SLOTS), 1)).astype(BF)


def pack_kernel(ids_ref, x_ref, g_ref, send_ref, slot_ref):
    ids = ids_ref[...]
    picked = iota((EXPERTS, TOK), 0) == ids
    before = (iota((TOK, TOK), 0) < iota((TOK, TOK), 1)).astype(BF)
    earlier = dot(picked.astype(BF), before, (1, 0))
    rank = jnp.sum(jnp.where(picked, earlier, 0.0), axis=0, keepdims=True).astype(jnp.int32)
    slot = ids * ROWS + rank
    slot_ref[...] = slot
    place = (iota((GRID, TOK), 0) == slot).astype(BF)
    both = jnp.concatenate([x_ref[...], g_ref[...]], axis=0)
    send_ref[...] = dot(place, both, (1, 1)).astype(BF)


def turn_kernel(me_ref, recv_ref, router_ref, out_ref):
    out_ref[: 2 * WID, :] = dot(recv_ref[...], slot_lanes(), (0, 0)).astype(BF)
    mine = (iota((16, EXPERTS), 1) == me_ref[0]).astype(BF)
    column = dot(mine, router_ref[...], (1, 0)).astype(BF)
    out_ref[2 * WID :, :] = jnp.concatenate([column, jnp.zeros((16, SLOTS - WID), BF)], axis=1)


def expert_kernel(core_ref, ag_ref, wg0, wg1, wu0, wu1, wd0, wd1, out_ref, x_ref, g_ref, r_ref, wg, wu, wd, sems):
    lanes = pl.ds(pl.multiple_of(core_ref[0] * 128, 128), 128)
    rest = pl.ds(256, 128)

    def cp(src, dst, k):
        c = pltpu.make_async_copy(src, dst, sems.at[k])
        c.start()
        return c

    def blocks(first, dst, k):
        got = []
        for j in range(N_ETP):
            rows, to = pl.ds(first, WID), pl.ds(j * WID, WID)
            got.append(cp(ag_ref.at[j, rows, lanes], dst.at[to, pl.ds(0, 128)], k + 2 * j))
            got.append(cp(ag_ref.at[j, rows, rest], dst.at[to, pl.ds(128, 128)], k + 2 * j + 1))
        return got

    n = 2 * N_ETP
    get_r = [cp(ag_ref.at[j, pl.ds(2 * WID, 16), pl.ds(0, 256)], r_ref.at[pl.ds(16 * j, 16)], 2 * n + j) for j in range(N_ETP)]
    get_x = blocks(0, x_ref, 0)
    k = 2 * n + N_ETP
    get_wg = [cp(w, wg.at[h], k + h) for h, w in enumerate((wg0, wg1))]
    get_wu = [cp(w, wu.at[h], k + 2 + h) for h, w in enumerate((wu0, wu1))]
    get_g = blocks(WID, g_ref, n)
    get_wd = [cp(w, wd.at[h], k + 4 + h) for h, w in enumerate((wd0, wd1))]

    for c in get_r + get_x:
        c.wait()
    x = x_ref[...]
    router = r_ref[...].astype(F32).T
    logit = jnp.zeros((1, 256), F32)
    for j in range(N_ETP):
        logit += jnp.sum(x_ref[pl.ds(j * WID, WID), :].astype(F32) * router[:WID, 16 * j : 16 * j + 1], axis=0, keepdims=True)
    score = 1.0 / (1.0 + jnp.exp(-logit))
    for c in get_wg:
        c.wait()
    gate = [dot(x, wg[h], (0, 0)).T for h in range(2)]
    for c in get_wu:
        c.wait()
    up = [dot(x, wu[h], (0, 0)).T for h in range(2)]
    for c in get_g + get_wd:
        c.wait()
    g = g_ref[...]
    d_gate, d_up = [], []
    d_score = jnp.zeros((1, 256), F32)
    for h in range(2):
        d_hidden = dot(wd[h], g, (1, 0))
        gate_pre, up_pre = gate[h] * score, up[h] * score
        sig = 1.0 / (1.0 + jnp.exp(-gate_pre))
        dg = (d_hidden * up_pre * (sig * (1.0 + gate_pre * (1.0 - sig)))).astype(BF)
        du = (d_hidden * (gate_pre * sig)).astype(BF)
        d_score += jnp.sum(dg.astype(F32) * gate[h] + du.astype(F32) * up[h], axis=0, keepdims=True)
        d_gate.append(dg)
        d_up.append(du)
    d_logit = d_score * score * (1.0 - score)
    keep = (iota((WID // 2, 128), 1) // 64) == core_ref[0]
    for j in range(N_ETP):
        rows = pl.ds(j * WID, WID)
        total = dot(wg[0, rows, :], d_gate[0], (1, 0)) + dot(wg[1, rows, :], d_gate[1], (1, 0))
        total += dot(wu[0, rows, :], d_up[0], (1, 0)) + dot(wu[1, rows, :], d_up[1], (1, 0))
        total = total * score + router[:WID, 16 * j : 16 * j + 1] * d_logit
        out_ref[j, :WID, :] = total[:, :128].astype(BF)
        top, bottom = total[: WID // 2, 128:], total[WID // 2 :, 128:]
        out_ref[j, WID:, :] = jnp.where(keep, top, pltpu.roll(bottom, 64, 1)).astype(BF)


def sum_kernel(recv_ref, out_ref):
    parts = []
    for c in range(2):
        total = recv_ref[c].astype(F32)
        for y in range(1, N_ETP // 2):
            total += recv_ref[2 * y + c].astype(F32)
        parts.append(total)
    first = iota((WID // 2, 128), 1) < 64
    top = jnp.where(first, parts[0][WID:], parts[1][WID:])
    bottom = jnp.where(first, pltpu.roll(parts[0][WID:], 64, 1), pltpu.roll(parts[1][WID:], 64, 1))
    whole = jnp.concatenate([parts[0][:WID], parts[1][:WID], jnp.concatenate([top, bottom], axis=0)], axis=1)
    out_ref[...] = dot(slot_lanes(), whole.astype(BF), (1, 1)).astype(BF)


def unpack_kernel(slot_ref, recv_ref, out_ref):
    place = (iota((GRID, TOK), 0) == slot_ref[...]).astype(BF)
    out_ref[...] = dot(recv_ref[...], place, (0, 0)).astype(BF)


VM = pl.BlockSpec(memory_space=pltpu.VMEM)
SM = pl.BlockSpec(memory_space=pltpu.SMEM)
ANY = pl.BlockSpec(memory_space=pl.ANY)


def call(kernel, ins, outs, out_specs=VM, scratch=(), vmem=32 << 20, cost=None):
    return pl.pallas_call(
        kernel,
        out_shape=outs,
        in_specs=ins,
        out_specs=out_specs,
        scratch_shapes=list(scratch),
        cost_estimate=cost,
        compiler_params=pltpu.CompilerParams(vmem_limit_bytes=vmem),
    )


def body(tokens, grad_out, expert_ids, router, gate_weight, up_weight, down_weight):
    me = lax.axis_index("ep").astype(jnp.int32).reshape(1)
    core = (lax.axis_index("etp") % 2).astype(jnp.int32).reshape(1)
    other = [(i, i ^ 1) for i in range(N_ETP)]
    own = [gate_weight[0], up_weight[0], down_weight[0]]
    shape = jax.ShapeDtypeStruct

    send, slot = call(pack_kernel, [VM] * 3, [shape((GRID, 2 * WID), BF), shape((1, TOK), jnp.int32)], [VM] * 2)(
        expert_ids.reshape(1, TOK), tokens.T, grad_out.T
    )
    recv = lax.all_to_all(send.reshape(EXPERTS, ROWS, 2 * WID), "ep", split_axis=0, concat_axis=0, tiled=True)
    turned = call(turn_kernel, [SM, VM, VM], shape((AG_ROWS, SLOTS), BF))(me, recv.reshape(GRID, 2 * WID), router.T)
    gathered = lax.all_gather(turned, "etp", axis=0, tiled=True).reshape(N_ETP, AG_ROWS, SLOTS)
    wg, wu, wd = own
    wg1, wu1, wd1 = (lax.ppermute(w, "etp", other) for w in own)
    partial = call(
        expert_kernel,
        [SM] + [ANY] * 7,
        shape((N_ETP, WID * 3 // 2, 128), BF),
        scratch=[
            pltpu.VMEM((D, 256), BF),
            pltpu.VMEM((D, 256), BF),
            pltpu.VMEM((256, 256), BF),
            pltpu.VMEM((2, D, HID), BF),
            pltpu.VMEM((2, D, HID), BF),
            pltpu.VMEM((2, HID, D), BF),
            pltpu.SemaphoreType.DMA((4 * N_ETP + N_ETP + 6,)),
        ],
        vmem=48 << 20,
        cost=pl.CostEstimate(flops=10 * D * 512 * 256, bytes_accessed=12 << 20, transcendentals=512 * 256),
    )(core, gathered, wg, wg1, wu, wu1, wd, wd1)
    parts = lax.all_to_all(partial, "etp", split_axis=0, concat_axis=0, tiled=True)
    summed = call(sum_kernel, [VM], shape((GRID, WID), BF))(parts)
    back = lax.all_to_all(summed.reshape(EXPERTS, ROWS, WID), "ep", split_axis=0, concat_axis=0, tiled=True)
    out = call(unpack_kernel, [VM] * 2, shape((WID, TOK), BF))(slot, back.reshape(GRID, WID))
    return out.T


def solution(mesh):
    placed = (
        P("ep", "etp"),
        P("ep", "etp"),
        P("ep", None),
        P("etp", None),
        P("ep", None, "etp"),
        P("ep", None, "etp"),
        P("ep", "etp", None),
    )
    return jax.shard_map(body, mesh=mesh, in_specs=placed, out_specs=P("ep", "etp"), check_vma=False)
```

time: 483 us -> 153 us (0.32)
  waiting for transfers between devices: 320 us -> 47.7 us
  local copies, waits for them, and re-layouts: 43.3 us -> 4.59 us
  matrix products: 19.6 us -> 0 us
  Pallas kernels: 0 us -> 11 us
  other arithmetic: 5.29 us -> 0 us
    all_to_all x3 -> x1, waiting for transfers between devices: 176 us -> 13.8 us  [body(): lax.all_to_all(send.reshape(EXPERTS, ROWS, 2 * WID), 'ep', split_axis=0,...]
    reduce_scatter x1 -> x0, waiting for transfers between devices: 62.2 us -> none  [body(): lax.psum_scatter(unpacked, 'etp', scatter_dimension=1, tiled=True)]
    psum x2 -> x0, blocking collectives: 55.2 us -> none  [the longest x1 29.8 us: body(): logit_sum = lax.psum(logit_part, 'etp')]
    all_to_all x0 -> x2, blocking collectives: none -> 53.6 us  [the longest x1 31.1 us: body(): lax.all_to_all(partial, 'etp', split_axis=0, concat_axis=0, tiled=True)]
    all_gather x2 -> x1, waiting for transfers between devices: 80.3 us -> 31 us  [body(): lax.all_gather(turned, 'etp', axis=0, tiled=True)]
    reshape x6 -> x0, local copies, waits for them, and re-layouts: 21 us -> none  [the longest x1 5.03 us: body(): unpacked = returned.reshape(experts * capacity, full_width)[slot_index]]
    dot_general x6 -> x0, matrix products: 19.6 us -> none  [the longest x4 15.7 us: contract_last(): lax.dot_general(left, right, (((1,), (1,)), ((), ())), preferred_element_...]
    all_to_all x3 -> x1, starting transfers between devices: 25.5 us -> 13.7 us  [body(): lax.all_to_all(send.reshape(EXPERTS, ROWS, 2 * WID), 'ep', split_axis=0,...]
  transfers between devices with their start and end apart: 6 -> 5, of which waited for: 6 -> 4; matrix products, arithmetic and copies ran while one was open for 3% -> 0% of each run, Pallas kernels for 0% -> 0%
where the time goes in v1:
time: 153 us
  blocking collectives  53.6 us (35%)
  waiting for transfers between devices  47.7 us (31%)
  starting transfers between devices  22.5 us (15%)
  between operations  13.5 us (9%)
  Pallas kernels  11 us (7%)
  local copies, waits for them, and re-layouts  4.59 us (3%)
    all_to_all x1, blocking collectives, body(): lax.all_to_all(partial, 'etp', split_axis=0, concat_axis=0, tiled=True)  31.1 us
    all_gather x1, waiting for transfers between devices, body(): lax.all_gather(turned, 'etp', axis=0, tiled=True)  31 us
    all_to_all x1, blocking collectives, body(): lax.all_to_all(summed.reshape(EXPERTS, ROWS, WID), 'ep', split_axis=0, co...  22.4 us
    all_to_all x1, waiting for transfers between devices, body(): lax.all_to_all(send.reshape(EXPERTS, ROWS, 2 * WID), 'ep', split_axis=0,...  13.8 us
    all_to_all x1, starting transfers between devices, body(): lax.all_to_all(send.reshape(EXPERTS, ROWS, 2 * WID), 'ep', split_axis=0,...  13.7 us
    ppermute x3, starting transfers between devices, body(): wg1, wu1, wd1 = (lax.ppermute(w, 'etp', other) for w in own)  8.74 us
    pallas_call x1, Pallas kernels, body(): call(expert_kernel, [SM] + [ANY] * 7, shape((N_ETP, WID * 3 // 2, 128), B...  7.4 us
    unnamed x12, local copies, waits for them, and re-layouts  4.59 us
  transfers between devices with their start and end apart: 5, of which 4 were waited for; matrix products, arithmetic and copies ran while one was open for 0% of the time, Pallas kernels for 0%

profile of v1, /device:TPU:1, one launch (start us, length us, event | category | flops | bytes accessed | tf_op | source)
XLA Modules:
  0.0 152.9 jit_solution(1676415556798536857)
XLA Ops:
  6.5 1.0 copy-done.2
  7.5 0.9 copy-done.3
  8.4 0.7 copy-done.5
  9.1 1.2 shard_map.73
  10.3 13.7 %all-to-all-start = ((bf16[32,16,320]{2,1,0:T(8,128)(2,1)}), bf16[32,16,320]{2,1,0:T(8,128)(2,1)S(1)}, u32[]{:S(2)}, u32[]{:S(2)}) async-start(bf16[32,16,320]{2,1,0:T(8,128)(2,1)} %bitcast.5), calls=%async_computation | async-start | bytes 786432 | tf_op jit(solution)/shard_map/all_to_all | solution.py:174
  24.0 0.0 all-gather.2.cloned.1.call-start
  24.1 13.8 %all-to-all-done = bf16[32,16,320]{2,1,0:T(8,128)(2,1)S(1)} async-done(((bf16[32,16,320]{2,1,0:T(8,128)(2,1)}), bf16[32,16,320]{2,1,0:T(8,128)(2,1)S(1)}, u32[]{:S(2)}, u32[]{:S(2)}) %all-to-all-start) | async-done | bytes 327712 | tf_op jit(solution)/shard_map/all_to_all | solution.py:174
  37.8 0.7 copy-done.4
  38.5 1.1 shard_map.74
  39.6 0.0 all-gather.2.cloned.1.call-update
  39.7 0.0 copy-done
  39.7 4.4 %collective-permute-start = (bf16[2560,256]{1,0:T(8,128)(2,1)S(1)}, bf16[2560,256]{1,0:T(8,128)(2,1)S(1)}, u32[]{:S(2)}, u32[]{:S(2)}) collective-permute-start(bf16[2560,256]{1,0:T(8,128)(2,1)S(1)} %bitcast.16), channel_id=1, source_target_pairs={{0,1},{1,0},{2,3},{3,2},{4,5},{5,4},{6,7},{7,6},{8,9},{9,8},{10,11... | collective-permute-start | bytes 3932168 | tf_op jit(solution)/shard_map/ppermute | solution.py:178
  44.1 1.9 %collective-permute-start.1 = (bf16[2560,256]{1,0:T(8,128)(2,1)}, bf16[2560,256]{1,0:T(8,128)(2,1)}, u32[]{:S(2)}, u32[]{:S(2)}) collective-permute-start(bf16[2560,256]{1,0:T(8,128)(2,1)} %bitcast.18), channel_id=1, source_target_pairs={{0,1},{1,0},{2,3},{3,2},{4,5},{5,4},{6,7},{7,6},{8,9},{9,8},{10,11... | collective-permute-start | bytes 3932168 | tf_op jit(solution)/shard_map/ppermute | solution.py:178
  46.0 2.4 %collective-permute-start.2 = (bf16[256,2560]{1,0:T(8,128)(2,1)}, bf16[256,2560]{1,0:T(8,128)(2,1)}, u32[]{:S(2)}, u32[]{:S(2)}) collective-permute-start(bf16[256,2560]{1,0:T(8,128)(2,1)} %bitcast.27), channel_id=1, source_target_pairs={{0,1},{1,0},{2,3},{3,2},{4,5},{5,4},{6,7},{7,6},{8,9},{9,8},{10,11... | collective-permute-start | bytes 3932168 | tf_op jit(solution)/shard_map/ppermute | solution.py:178
  48.4 0.0 collective-permute-done.wg1
  48.4 0.9 collective-permute-done.1.wu1
  49.4 2.1 %collective-permute-done.2.wd1 = bf16[256,2560]{1,0:T(8,128)(2,1)} collective-permute-done((bf16[256,2560]{1,0:T(8,128)(2,1)}, bf16[256,2560]{1,0:T(8,128)(2,1)}, u32[]{:S(2)}, u32[]{:S(2)}) %collective-permute-start.2) | collective-permute-done | bytes 1310752 | tf_op jit(solution)/shard_map/ppermute | solution.py:178
  51.4 31.0 %all-gather.2.cloned.1.call-done = bf16[5376,384]{1,0:T(8,128)(2,1)} async-done(((bf16[336,384]{1,0:T(8,128)(2,1)}), bf16[5376,384]{1,0:T(8,128)(2,1)}) %all-gather.2.cloned.1.call-update) | async-done | bytes 4128784 | tf_op jit(solution)/shard_map/all_gather | solution.py:176
  82.4 1.3 copy-done.1
  83.7 7.4 %shard_map.75 = bf16[16,240,128]{2,1,0:T(8,128)(2,1)S(1)} custom-call(s32[1]{0:T(128)} %bitcast.3.core_ref, bf16[16,336,384]{2,1,0:T(8,128)(2,1)} %bitcast.26, bf16[2560,256]{1,0:T(8,128)(2,1)S(1)} %bitcast.17, bf16[2560,256]{1,0:T(8,128)(2,1)S(1)} %collective-permute-done.wg1, bf16[2560,256]{1,0:T(8,128)(2,1)S(1)} %bitcast.19, ...), custom_call_target="tpu_custom_call" | custom-call | flops 3355443200 | bytes 12582912 | tf_op jit(solution)/shard_map/pallas_call | solution.py:179
  91.1 31.1 %all_to_all.15.recv_ref = bf16[16,240,128]{2,1,0:T(8,128)(2,1)S(1)} all-to-all(bf16[16,240,128]{2,1,0:T(8,128)(2,1)S(1)} %shard_map.75), channel_id=1, replica_groups=mesh['ep'=32,'etp'=16] {'etp'}, dimensions={0} | all-to-all | bytes 1966080 | tf_op jit(solution)/shard_map/all_to_all | solution.py:195
  122.3 0.4 shard_map.76
  122.7 22.4 %all_to_all.16 = bf16[32,16,160]{2,1,0:T(8,128)(2,1)S(1)} all-to-all(bf16[32,16,160]{2,1,0:T(8,128)(2,1)S(1)} %bitcast.20), channel_id=1, replica_groups=mesh['ep'=32,'etp'=16] {'ep'}, dimensions={0} | all-to-all | bytes 327680 | tf_op jit(solution)/shard_map/all_to_all | solution.py:197
  145.1 0.9 shard_map.77
  (6 shorter events, 0.0 us)
Async XLA Ops:
  6.5 33.1 %copy-start = (bf16[1,2560,256]{2,1,0:T(8,128)(2,1)S(1)}, bf16[1,2560,256]{2,1,0:T(8,128)(2,1)}, u32[]{:S(2)}) copy-start(bf16[1,2560,256]{2,1,0:T(8,128)(2,1)} %param.11) | copy-start | bytes 3932164
  6.5 1.0 copy-start.2
  7.5 0.9 copy-start.3
  8.4 0.7 copy-start.5
  10.3 27.5 %all-to-all-start = ((bf16[32,16,320]{2,1,0:T(8,128)(2,1)}), bf16[32,16,320]{2,1,0:T(8,128)(2,1)S(1)}, u32[]{:S(2)}, u32[]{:S(2)}) async-start(bf16[32,16,320]{2,1,0:T(8,128)(2,1)} %bitcast.5), calls=%async_computation | async-start | bytes 786432 | tf_op jit(solution)/shard_map/all_to_all | solution.py:174
  24.0 58.4 %all-gather.2.cloned.1.call-start = ((), (), s32[]{:S(2)}) async-start(), calls=%async_computation.3 | async-start | bytes 4386816 | tf_op jit(solution)/shard_map/all_gather | solution.py:176
  37.8 0.7 copy-start.4
  39.7 8.8 %collective-permute-start = (bf16[2560,256]{1,0:T(8,128)(2,1)S(1)}, bf16[2560,256]{1,0:T(8,128)(2,1)S(1)}, u32[]{:S(2)}, u32[]{:S(2)}) collective-permute-start(bf16[2560,256]{1,0:T(8,128)(2,1)S(1)} %bitcast.16), channel_id=1, source_target_pairs={{0,1},{1,0},{2,3},{3,2},{4,5},{5,4},{6,7},{7,6},{8,9},{9,8},{10,11... | collective-permute-start | bytes 3932168 | tf_op jit(solution)/shard_map/ppermute | solution.py:178
  44.1 5.3 %collective-permute-start.1 = (bf16[2560,256]{1,0:T(8,128)(2,1)}, bf16[2560,256]{1,0:T(8,128)(2,1)}, u32[]{:S(2)}, u32[]{:S(2)}) collective-permute-start(bf16[2560,256]{1,0:T(8,128)(2,1)} %bitcast.18), channel_id=1, source_target_pairs={{0,1},{1,0},{2,3},{3,2},{4,5},{5,4},{6,7},{7,6},{8,9},{9,8},{10,11... | collective-permute-start | bytes 3932168 | tf_op jit(solution)/shard_map/ppermute | solution.py:178
  46.0 5.4 %collective-permute-start.2 = (bf16[256,2560]{1,0:T(8,128)(2,1)}, bf16[256,2560]{1,0:T(8,128)(2,1)}, u32[]{:S(2)}, u32[]{:S(2)}) collective-permute-start(bf16[256,2560]{1,0:T(8,128)(2,1)} %bitcast.27), channel_id=1, source_target_pairs={{0,1},{1,0},{2,3},{3,2},{4,5},{5,4},{6,7},{7,6},{8,9},{9,8},{10,11... | collective-permute-start | bytes 3932168 | tf_op jit(solution)/shard_map/ppermute | solution.py:178
  82.4 1.3 copy-start.1
Sparse Core Ops, SparseCore 0:
  39.8 42.5 all-gather.1

commit v2 on v1

v2 whole, which is shorter than its diff:
```python
import jax
import jax.numpy as jnp
from jax import lax
from jax.experimental import pallas as pl
from jax.experimental.pallas import tpu as pltpu
from jax.sharding import PartitionSpec as P

CAP = 12
ROWS = 16
EXPERTS = 32
TOK = 256
WID = 160
N_ETP = 16
D = WID * N_ETP
HID = 256
SLOTS = EXPERTS * CAP
HALF = SLOTS // 2
GRID = EXPERTS * ROWS
AG_ROWS = 2 * WID + 8
F32 = jnp.float32
BF = jnp.bfloat16


def iota(shape, dim):
    return lax.broadcasted_iota(jnp.int32, shape, dim)


def dot(left, right, dims):
    return lax.dot_general(left, right, ((dims[:1], dims[1:]), ((), ())), preferred_element_type=F32)


def slot_lanes():
    row = iota((GRID, 1), 0)
    src, rank = row // ROWS, row % ROWS
    half = src // (EXPERTS // 2)
    at = (src % (EXPERTS // 2)) * CAP + rank
    lane = jnp.where(at < 128, half * 128 + at, 256 + half * 64 + at - 128)
    lane = jnp.where(rank < CAP, lane, -1)
    return (lane == iota((GRID, SLOTS), 1)).astype(BF)


def power(k):
    size, out = jnp.abs(k).astype(jnp.int32), jnp.ones_like(k)
    for bit in range(7):
        factor = jnp.where(k < 0, 2.0 ** -(1 << bit), 2.0 ** (1 << bit))
        out = jnp.where((size & (1 << bit)) != 0, out * factor, out)
    return out


def level(top):
    return 14.0 - jnp.clip(jnp.floor(jnp.log2(jnp.maximum(top, 1e-36))), -110.0, 14.0)


def pack_kernel(ids_ref, x_ref, g_ref, send_ref, slot_ref, ids_v, x_v, g_v, sems):
    copies = [
        pltpu.make_async_copy(src, dst, sems.at[i])
        for i, (src, dst) in enumerate(((ids_ref, ids_v), (x_ref, x_v), (g_ref, g_v)))
    ]
    for c in copies:
        c.start()
    for c in copies:
        c.wait()
    ids = ids_v[...]
    picked = iota((EXPERTS, TOK), 0) == ids
    before = (iota((TOK, TOK), 0) < iota((TOK, TOK), 1)).astype(BF)
    earlier = dot(picked.astype(BF), before, (1, 0))
    rank = jnp.sum(jnp.where(picked, earlier, 0.0), axis=0, keepdims=True).astype(jnp.int32)
    slot = ids * ROWS + rank
    slot_ref[...] = slot
    place = (iota((GRID, TOK), 0) == slot).astype(BF)
    both = jnp.concatenate([x_v[...], g_v[...]], axis=0)
    send_ref[...] = dot(place, both, (1, 1)).astype(BF)


def router_kernel(me_ref, router_ref, out_ref):
    mine = (iota((8, EXPERTS), 1) == me_ref[0]).astype(BF)
    column = dot(mine, router_ref[...], (1, 0))
    shift = level(jnp.max(jnp.abs(column), axis=1, keepdims=True))
    scaled = column * power(shift)
    row = jnp.concatenate([scaled[:, :128], scaled[:, :128], scaled[:, 128:], jnp.zeros((8, 96), F32)], axis=1)
    out_ref[...] = jnp.where(iota((8, SLOTS), 0) == 0, row, jnp.broadcast_to(shift, (8, SLOTS)))


def turn_kernel(recv_ref, router_ref, out_ref):
    both = dot(recv_ref[...], slot_lanes(), (0, 0))
    shifts = []
    for i in range(2):
        half = both[i * WID : (i + 1) * WID]
        shift = level(jnp.max(jnp.abs(half), axis=0, keepdims=True))
        out_ref[i * WID : (i + 1) * WID, :] = half * power(shift)
        shifts.append(shift)
    row = iota((8, SLOTS), 0)
    out_ref[2 * WID :, :] = jnp.where(row < 2, router_ref[...], jnp.where(row == 2, shifts[0], shifts[1]))


def expert_kernel(core_ref, lo_ref, hi_ref, wg0, wu0, wd_other, wg_own, wu_own, wd_own, out_ref, x_ref, g_ref, wd0, wg1, wu1, wd1, sems):
    copies = [
        pltpu.make_async_copy(src, dst, sems.at[i])
        for i, (src, dst) in enumerate(((wd_other, wd0), (wg_own, wg1), (wu_own, wu1), (wd_own, wd1)))
    ]
    for c in copies:
        c.start()

    def rows(first, count):
        return jnp.concatenate([lo_ref[:, first : first + count, :], hi_ref[:, first : first + count, :]], axis=2)

    extra = rows(2 * WID, 8).astype(F32)
    back = power(-extra)
    logit = jnp.zeros((1, 256), F32)
    columns = []
    for j in range(N_ETP):
        at = pl.ds(j * WID, WID)
        for first, ref, row in ((0, x_ref, 2), (WID, g_ref, 3)):
            scale = back[j, row : row + 1, :].astype(BF)
            ref[at, :128] = lo_ref[j, first : first + WID, :] * scale[:, :128]
            ref[at, 128:] = hi_ref[j, first : first + WID, :] * scale[:, 128:]
        line = (extra[j, :8] * back[j, 1:2])[:, :WID]
        column = line.T[:, :1]
        logit += jnp.sum(x_ref[at, :].astype(F32) * column, axis=0, keepdims=True)
        columns.append(column)
    score = 1.0 / (1.0 + jnp.exp(-logit))
    xt = x_ref[...].T
    g = g_ref[...]
    d_gate, d_up = [], []
    d_score = jnp.zeros((1, 256), F32)
    for h, (wg, wu, wd) in enumerate(((wg0, wu0, wd0), (wg1, wu1, wd1))):
        for c in copies[1:] if h else copies[:1]:
            c.wait()
        gate = dot(xt, wg[...], (1, 0)).T
        up = dot(xt, wu[...], (1, 0)).T
        d_hidden = dot(wd[...], g, (1, 0))
        gate_pre, up_pre = gate * score, up * score
        sig = 1.0 / (1.0 + jnp.exp(-gate_pre))
        dg = (d_hidden * up_pre * (sig * (1.0 + gate_pre * (1.0 - sig)))).astype(BF)
        du = (d_hidden * (gate_pre * sig)).astype(BF)
        d_score += jnp.sum(dg.astype(F32) * gate + du.astype(F32) * up, axis=0, keepdims=True)
        d_gate.append(dg)
        d_up.append(du)
    d_logit = d_score * score * (1.0 - score)
    keep = (iota((WID // 2, 128), 1) // 64) == core_ref[0]
    for j in range(N_ETP):
        at = pl.ds(j * WID, WID)
        total = dot(wg0[at, :], d_gate[0], (1, 0)) + dot(wg1[at, :], d_gate[1], (1, 0))
        total += dot(wu0[at, :], d_up[0], (1, 0)) + dot(wu1[at, :], d_up[1], (1, 0))
        total = total * score + columns[j] * d_logit
        out_ref[j, :WID, :] = total[:, :128].astype(BF)
        top, bottom = total[: WID // 2, 128:], total[WID // 2 :, 128:]
        out_ref[j, WID:, :] = jnp.where(keep, top, pltpu.roll(bottom, 64, 1)).astype(BF)


def sum_kernel(recv_ref, out_ref):
    parts = []
    for c in range(2):
        total = recv_ref[c].astype(F32)
        for y in range(1, N_ETP // 2):
            total += recv_ref[2 * y + c].astype(F32)
        parts.append(total)
    first = iota((WID // 2, 128), 1) < 64
    top = jnp.where(first, parts[0][WID:], parts[1][WID:])
    bottom = jnp.where(first, pltpu.roll(parts[0][WID:], 64, 1), pltpu.roll(parts[1][WID:], 64, 1))
    whole = jnp.concatenate([parts[0][:WID], parts[1][:WID], jnp.concatenate([top, bottom], axis=0)], axis=1)
    out_ref[...] = dot(slot_lanes(), whole.astype(BF), (1, 1)).astype(BF)


def unpack_kernel(slot_ref, recv_ref, out_ref):
    place = (iota((GRID, TOK), 0) == slot_ref[...]).astype(BF)
    out_ref[...] = dot(recv_ref[...], place, (0, 0)).astype(BF)


VM = pl.BlockSpec(memory_space=pltpu.VMEM)
SM = pl.BlockSpec(memory_space=pltpu.SMEM)
HBM = pl.BlockSpec(memory_space=pltpu.HBM)


def in_hbm(x):
    return pltpu.with_memory_space_constraint(x, pltpu.HBM)


def call(kernel, ins, outs, out_specs=VM, scratch=(), vmem=32 << 20, cost=None):
    return pl.pallas_call(
        kernel,
        out_shape=outs,
        in_specs=ins,
        out_specs=out_specs,
        scratch_shapes=list(scratch),
        cost_estimate=cost,
        compiler_params=pltpu.CompilerParams(vmem_limit_bytes=vmem),
    )


def body(tokens, grad_out, expert_ids, router, gate_weight, up_weight, down_weight):
    me = lax.axis_index("ep").astype(jnp.int32).reshape(1)
    core = (lax.axis_index("etp") % 2).astype(jnp.int32).reshape(1)
    other = [(i, i ^ 1) for i in range(N_ETP)]
    own = [gate_weight[0], up_weight[0], down_weight[0]]
    shape = jax.ShapeDtypeStruct

    send, slot = call(
        pack_kernel,
        [HBM] * 3,
        [shape((GRID, 2 * WID), BF), shape((1, TOK), jnp.int32)],
        [VM] * 2,
        [pltpu.VMEM((1, TOK), jnp.int32), pltpu.VMEM((WID, TOK), BF), pltpu.VMEM((WID, TOK), BF), pltpu.SemaphoreType.DMA((3,))],
    )(in_hbm(expert_ids.reshape(1, TOK)), in_hbm(tokens.T), in_hbm(grad_out.T))
    line = call(router_kernel, [SM, VM], shape((8, SLOTS), F32))(me, router.T)
    recv = lax.all_to_all(send.reshape(EXPERTS, ROWS, 2 * WID), "ep", split_axis=0, concat_axis=0, tiled=True)
    turned = call(turn_kernel, [VM, VM], shape((AG_ROWS, SLOTS), F32))(recv.reshape(GRID, 2 * WID), line)
    gathered = lax.all_gather(turned.astype(jnp.float16), "etp", axis=0, tiled=True).reshape(N_ETP, AG_ROWS, SLOTS)
    lo = lax.dynamic_slice(gathered, (0, 0, 128 * core[0]), (N_ETP, AG_ROWS, 128)).astype(BF)
    hi = gathered[:, :, 256:].astype(BF)
    wg, wu, wd = own
    wg1, wu1, wd1 = (lax.ppermute(w, "etp", other) for w in own)
    partial = call(
        expert_kernel,
        [SM] + [VM] * 4 + [HBM] * 4,
        shape((N_ETP, WID * 3 // 2, 128), BF),
        scratch=[
            pltpu.VMEM((D, 256), BF),
            pltpu.VMEM((D, 256), BF),
            pltpu.VMEM((HID, D), BF),
            pltpu.VMEM((D, HID), BF),
            pltpu.VMEM((D, HID), BF),
            pltpu.VMEM((HID, D), BF),
            pltpu.SemaphoreType.DMA((4,)),
        ],
        vmem=24 << 20,
        cost=pl.CostEstimate(flops=10 * D * 512 * 256, bytes_accessed=12 << 20, transcendentals=512 * 256),
    )(core, lo, hi, wg1, wu1, *map(in_hbm, (wd1, wg, wu, wd)))
    parts = lax.all_to_all(partial, "etp", split_axis=0, concat_axis=0, tiled=True)
    summed = call(sum_kernel, [VM], shape((GRID, WID), BF))(parts)
    back = lax.all_to_all(summed.reshape(EXPERTS, ROWS, WID), "ep", split_axis=0, concat_axis=0, tiled=True)
    out = call(unpack_kernel, [VM] * 2, shape((WID, TOK), BF))(slot, back.reshape(GRID, WID))
    return out.T


def solution(mesh):
    placed = (
        P("ep", "etp"),
        P("ep", "etp"),
        P("ep", None),
        P("etp", None),
        P("ep", None, "etp"),
        P("ep", None, "etp"),
        P("ep", "etp", None),
    )
    return jax.shard_map(body, mesh=mesh, in_specs=placed, out_specs=P("ep", "etp"), check_vma=False)
```

time: 153 us -> 123 us (0.80)
  waiting for transfers between devices: 47.7 us -> 5.63 us
  blocking collectives: 53.6 us -> 83.5 us
  between operations: 13.5 us -> 0.13 us
  local copies, waits for them, and re-layouts: 4.59 us -> 0.71 us
  starting transfers between devices: 22.5 us -> 20.9 us
    all_gather x0 -> x1, blocking collectives: none -> 34.4 us  [body(): lax.all_gather(turned.astype(jnp.float16), 'etp', axis=0, tiled=True)]
    all_gather x1 -> x0, waiting for transfers between devices: 31 us -> none  [body(): lax.all_gather(turned, 'etp', axis=0, tiled=True)]
    all_to_all x1, waiting for transfers between devices: 13.8 us -> 5.62 us  [body(): lax.all_to_all(send.reshape(EXPERTS, ROWS, 2 * WID), 'ep', split_axis=0,...]
    all_to_all x1, blocking collectives: 22.4 us -> 16.6 us  [body(): lax.all_to_all(summed.reshape(EXPERTS, ROWS, WID), 'ep', split_axis=0, co...]
    unnamed x12 -> x2, local copies, waits for them, and re-layouts: 4.59 us -> 0.71 us
    ppermute x3, waiting for transfers between devices: 2.96 us -> 0.01 us  [body(): wg1, wu1, wd1 = (lax.ppermute(w, 'etp', other) for w in own)]
    ppermute x3, starting transfers between devices: 8.74 us -> 7.19 us  [body(): wg1, wu1, wd1 = (lax.ppermute(w, 'etp', other) for w in own)]
    pallas_call x3 -> x4, Pallas kernels: 9.69 us -> 10 us  [the longest x1 7.18 us: body(): call(expert_kernel, [SM] + [VM] * 4 + [HBM] * 4, shape((N_ETP, WID * 3 //...]
  transfers between devices with their start and end apart: 5 -> 4, of which waited for: 4 -> 1; matrix products, arithmetic and copies ran while one was open for 0% -> 0% of each run, Pallas kernels for 0% -> 1%
where the time goes in v2:
time: 123 us
  blocking collectives  83.5 us (68%)
  starting transfers between devices  20.9 us (17%)
  Pallas kernels  11.3 us (9%)
  waiting for transfers between devices  5.63 us (5%)
    all_gather x1, blocking collectives, body(): lax.all_gather(turned.astype(jnp.float16), 'etp', axis=0, tiled=True)  34.4 us
    all_to_all x1, blocking collectives, body(): lax.all_to_all(partial, 'etp', split_axis=0, concat_axis=0, tiled=True)  32.6 us
    all_to_all x1, blocking collectives, body(): lax.all_to_all(summed.reshape(EXPERTS, ROWS, WID), 'ep', split_axis=0, co...  16.6 us
    all_to_all x1, starting transfers between devices, body(): lax.all_to_all(send.reshape(EXPERTS, ROWS, 2 * WID), 'ep', split_axis=0,...  13.7 us
    ppermute x3, starting transfers between devices, body(): wg1, wu1, wd1 = (lax.ppermute(w, 'etp', other) for w in own)  7.19 us
    pallas_call x1, Pallas kernels, body(): call(expert_kernel, [SM] + [VM] * 4 + [HBM] * 4, shape((N_ETP, WID * 3 //...  7.18 us
    all_to_all x1, waiting for transfers between devices, body(): lax.all_to_all(send.reshape(EXPERTS, ROWS, 2 * WID), 'ep', split_axis=0,...  5.62 us
  transfers between devices with their start and end apart: 4, of which 1 were waited for; matrix products, arithmetic and copies ran while one was open for 0% of the time, Pallas kernels for 1%

profile of v2, /device:TPU:1, one launch (start us, length us, event | category | flops | bytes accessed | tf_op | source)
XLA Modules:
  0.0 122.8 jit_solution(445400581773456221)
XLA Ops:
  0.0 2.2 %shard_map.73 = (bf16[512,320]{1,0:T(8,128)(2,1)}, s32[1,256]{1,0:T(1,128)S(1)}) custom-call(s32[1,256]{1,0:T(1,128)} %bitcast.22, bf16[160,256]{1,0:T(8,128)(2,1)} %bitcast.20, bf16[160,256]{1,0:T(8,128)(2,1)} %bitcast.21), custom_call_target="tpu_custom_call" | custom-call | tf_op jit(solution)/shard_map/pallas_call | solution.py:198
  2.2 13.7 %all-to-all-start = ((bf16[32,16,320]{2,1,0:T(8,128)(2,1)}), bf16[32,16,320]{2,1,0:T(8,128)(2,1)S(1)}, u32[]{:S(2)}, u32[]{:S(2)}) async-start(bf16[32,16,320]{2,1,0:T(8,128)(2,1)} %bitcast.4), calls=%async_computation | async-start | bytes 786432 | tf_op jit(solution)/shard_map/all_to_all | solution.py:206
  15.9 2.9 %collective-permute-start = (bf16[2560,256]{1,0:T(8,128)(2,1)}, bf16[2560,256]{1,0:T(8,128)(2,1)S(1)}, u32[]{:S(2)}, u32[]{:S(2)}) collective-permute-start(bf16[2560,256]{1,0:T(8,128)(2,1)} %bitcast.23), channel_id=1, source_target_pairs={{0,1},{1,0},{2,3},{3,2},{4,5},{5,4},{6,7},{7,6},{8,9},{9,8},{10,11... | collective-permute-start | bytes 3932168 | tf_op jit(solution)/shard_map/ppermute | solution.py:212
  18.8 1.9 %collective-permute-start.1 = (bf16[2560,256]{1,0:T(8,128)(2,1)}, bf16[2560,256]{1,0:T(8,128)(2,1)S(1)}, u32[]{:S(2)}, u32[]{:S(2)}) collective-permute-start(bf16[2560,256]{1,0:T(8,128)(2,1)} %bitcast.25), channel_id=1, source_target_pairs={{0,1},{1,0},{2,3},{3,2},{4,5},{5,4},{6,7},{7,6},{8,9},{9,8},{10,11... | collective-permute-start | bytes 3932168 | tf_op jit(solution)/shard_map/ppermute | solution.py:212
  20.7 2.4 %collective-permute-start.2 = (bf16[256,2560]{1,0:T(8,128)(2,1)}, bf16[256,2560]{1,0:T(8,128)(2,1)}, u32[]{:S(2)}, u32[]{:S(2)}) collective-permute-start(bf16[256,2560]{1,0:T(8,128)(2,1)} %bitcast.27), channel_id=1, source_target_pairs={{0,1},{1,0},{2,3},{3,2},{4,5},{5,4},{6,7},{7,6},{8,9},{9,8},{10,11... | collective-permute-start | bytes 3932168 | tf_op jit(solution)/shard_map/ppermute | solution.py:212
  23.1 0.0 copy-start
  23.2 0.7 copy-done
  23.9 0.2 shard_map.74.router_ref
  24.1 5.6 %all-to-all-done = bf16[32,16,320]{2,1,0:T(8,128)(2,1)S(1)} async-done(((bf16[32,16,320]{2,1,0:T(8,128)(2,1)}), bf16[32,16,320]{2,1,0:T(8,128)(2,1)S(1)}, u32[]{:S(2)}, u32[]{:S(2)}) %all-to-all-start) | async-done | bytes 327712 | tf_op jit(solution)/shard_map/all_to_all | solution.py:206
  29.7 0.5 shard_map.75
  30.2 34.4 %all-gather.1 = f16[5248,384]{1,0:T(8,128)(2,1)S(1)} all-gather(f16[328,384]{1,0:T(8,128)(2,1)S(1)} %convert_element_type.9), channel_id=1, replica_groups=mesh['ep'=32,'etp'=16] {'etp'}, dimensions={0}, use_global_device_ids=true | all-gather | bytes 4282368 | tf_op jit(solution)/shard_map/all_gather | solution.py:208
  64.6 0.5 slice_convert_fusion
  65.1 0.0 collective-permute-done.wg0
  65.1 0.0 collective-permute-done.1.wu0
  65.1 0.0 collective-permute-done.2.wd_other
  65.1 7.2 %shard_map.76 = bf16[16,240,128]{2,1,0:T(8,128)(2,1)S(1)} custom-call(s32[1]{0:T(128)} %bitcast.3.core_ref, bf16[16,328,128]{2,1,0:T(8,128)(2,1)S(1)} %get-tuple-element.10.lo_ref, bf16[16,328,128]{2,1,0:T(8,128)(2,1)S(1)} %get-tuple-element.9.hi_ref, bf16[2560,256]{1,0:T(8,128)(2,1)S(1)} %collective-permute-done.wg0, ...), custom_call_target="tpu_custom_call" | custom-call | flops 3355443200 | bytes 12582912 | tf_op jit(solution)/shard_map/pallas_call | solution.py:213
  72.3 32.6 %all_to_all.15.recv_ref = bf16[16,240,128]{2,1,0:T(8,128)(2,1)S(1)} all-to-all(bf16[16,240,128]{2,1,0:T(8,128)(2,1)S(1)} %shard_map.76), channel_id=1, replica_groups=mesh['ep'=32,'etp'=16] {'etp'}, dimensions={0} | all-to-all | bytes 1966080 | tf_op jit(solution)/shard_map/all_to_all | solution.py:229
  104.9 0.4 shard_map.77
  105.3 16.6 %all_to_all.16 = bf16[32,16,160]{2,1,0:T(8,128)(2,1)S(1)} all-to-all(bf16[32,16,160]{2,1,0:T(8,128)(2,1)S(1)} %bitcast.16), channel_id=1, replica_groups=mesh['ep'=32,'etp'=16] {'ep'}, dimensions={0} | all-to-all | bytes 327680 | tf_op jit(solution)/shard_map/all_to_all | solution.py:231
  121.9 0.9 shard_map.78
  (1 shorter events, 0.0 us)
Async XLA Ops:
  2.2 27.5 %all-to-all-start = ((bf16[32,16,320]{2,1,0:T(8,128)(2,1)}), bf16[32,16,320]{2,1,0:T(8,128)(2,1)S(1)}, u32[]{:S(2)}, u32[]{:S(2)}) async-start(bf16[32,16,320]{2,1,0:T(8,128)(2,1)} %bitcast.4), calls=%async_computation | async-start | bytes 786432 | tf_op jit(solution)/shard_map/all_to_all | solution.py:206
  15.9 49.2 %collective-permute-start = (bf16[2560,256]{1,0:T(8,128)(2,1)}, bf16[2560,256]{1,0:T(8,128)(2,1)S(1)}, u32[]{:S(2)}, u32[]{:S(2)}) collective-permute-start(bf16[2560,256]{1,0:T(8,128)(2,1)} %bitcast.23), channel_id=1, source_target_pairs={{0,1},{1,0},{2,3},{3,2},{4,5},{5,4},{6,7},{7,6},{8,9},{9,8},{10,11... | collective-permute-start | bytes 3932168 | tf_op jit(solution)/shard_map/ppermute | solution.py:212
  18.8 46.3 %collective-permute-start.1 = (bf16[2560,256]{1,0:T(8,128)(2,1)}, bf16[2560,256]{1,0:T(8,128)(2,1)S(1)}, u32[]{:S(2)}, u32[]{:S(2)}) collective-permute-start(bf16[2560,256]{1,0:T(8,128)(2,1)} %bitcast.25), channel_id=1, source_target_pairs={{0,1},{1,0},{2,3},{3,2},{4,5},{5,4},{6,7},{7,6},{8,9},{9,8},{10,11... | collective-permute-start | bytes 3932168 | tf_op jit(solution)/shard_map/ppermute | solution.py:212
  20.7 44.4 %collective-permute-start.2 = (bf16[256,2560]{1,0:T(8,128)(2,1)}, bf16[256,2560]{1,0:T(8,128)(2,1)}, u32[]{:S(2)}, u32[]{:S(2)}) collective-permute-start(bf16[256,2560]{1,0:T(8,128)(2,1)} %bitcast.27), channel_id=1, source_target_pairs={{0,1},{1,0},{2,3},{3,2},{4,5},{5,4},{6,7},{7,6},{8,9},{9,8},{10,11... | collective-permute-start | bytes 3932168 | tf_op jit(solution)/shard_map/ppermute | solution.py:212
  23.1 0.7 copy-start

commit v3 on v2

--- a/solution.py
+++ b/solution.py
@@ -29,14 +29,16 @@
     return lax.dot_general(left, right, ((dims[:1], dims[1:]), ((), ())), preferred_element_type=F32)
 
 
+def lane_slots():
+    lane = iota((1, SLOTS), 1)
+    half = jnp.where(lane < 256, lane // 128, lane // 64 % 2)
+    at = jnp.where(lane < 256, lane % 128, 128 + lane % 64)
+    return half * (EXPERTS // 2) + at // CAP, at % CAP
+
+
 def slot_lanes():
-    row = iota((GRID, 1), 0)
-    src, rank = row // ROWS, row % ROWS
-    half = src // (EXPERTS // 2)
-    at = (src % (EXPERTS // 2)) * CAP + rank
-    lane = jnp.where(at < 128, half * 128 + at, 256 + half * 64 + at - 128)
-    lane = jnp.where(rank < CAP, lane, -1)
-    return (lane == iota((GRID, SLOTS), 1)).astype(BF)
+    src, rank = lane_slots()
+    return (iota((GRID, SLOTS), 0) == src * ROWS + rank).astype(BF)
 
 
 def power(k):
@@ -51,15 +53,21 @@
     return 14.0 - jnp.clip(jnp.floor(jnp.log2(jnp.maximum(top, 1e-36))), -110.0, 14.0)
 
 
-def pack_kernel(ids_ref, x_ref, g_ref, send_ref, slot_ref, ids_v, x_v, g_v, sems):
+def pack_kernel(me_ref, ids_ref, x_ref, g_ref, router_ref, send_ref, slot_ref, line_ref, ids_v, x_v, g_v, router_v, sems):
     copies = [
         pltpu.make_async_copy(src, dst, sems.at[i])
-        for i, (src, dst) in enumerate(((ids_ref, ids_v), (x_ref, x_v), (g_ref, g_v)))
+        for i, (src, dst) in enumerate(((ids_ref, ids_v), (x_ref, x_v), (g_ref, g_v), (router_ref, router_v)))
     ]
     for c in copies:
         c.start()
     for c in copies:
         c.wait()
+    mine = (iota((8, EXPERTS), 1) == me_ref[0]).astype(BF)
+    column = dot(mine, router_v[...], (1, 0))
+    shift = level(jnp.max(jnp.abs(column), axis=1, keepdims=True))
+    scaled = column * power(shift)
+    row = jnp.concatenate([scaled[:, :128], scaled[:, :128], scaled[:, 128:], jnp.zeros((8, 96), F32)], axis=1)
+    line_ref[...] = jnp.where(iota((8, SLOTS), 0) == 0, row, jnp.broadcast_to(shift, (8, SLOTS)))
     ids = ids_v[...]
     picked = iota((EXPERTS, TOK), 0) == ids
     before = (iota((TOK, TOK), 0) < iota((TOK, TOK), 1)).astype(BF)
@@ -72,15 +80,6 @@
     send_ref[...] = dot(place, both, (1, 1)).astype(BF)
 
 
-def router_kernel(me_ref, router_ref, out_ref):
-    mine = (iota((8, EXPERTS), 1) == me_ref[0]).astype(BF)
-    column = dot(mine, router_ref[...], (1, 0))
-    shift = level(jnp.max(jnp.abs(column), axis=1, keepdims=True))
-    scaled = column * power(shift)
-    row = jnp.concatenate([scaled[:, :128], scaled[:, :128], scaled[:, 128:], jnp.zeros((8, 96), F32)], axis=1)
-    out_ref[...] = jnp.where(iota((8, SLOTS), 0) == 0, row, jnp.broadcast_to(shift, (8, SLOTS)))
-
-
 def turn_kernel(recv_ref, router_ref, out_ref):
     both = dot(recv_ref[...], slot_lanes(), (0, 0))
     shifts = []
@@ -94,12 +93,14 @@
 
 
 def expert_kernel(core_ref, lo_ref, hi_ref, wg0, wu0, wd_other, wg_own, wu_own, wd_own, out_ref, x_ref, g_ref, wd0, wg1, wu1, wd1, sems):
-    copies = [
-        pltpu.make_async_copy(src, dst, sems.at[i])
-        for i, (src, dst) in enumerate(((wd_other, wd0), (wg_own, wg1), (wu_own, wu1), (wd_own, wd1)))
-    ]
-    for c in copies:
-        c.start()
+    copies = []
+    for i, (src, dst) in enumerate(((wd_other, wd0), (wg_own, wg1), (wu_own, wu1), (wd_own, wd1))):
+        size = dst.shape[0] // 2
+        parts = [pl.ds(p * size, size) for p in range(2)]
+        copies.append([pltpu.make_async_copy(src.at[at], dst.at[at], sems.at[i, p]) for p, at in enumerate(parts)])
+    for group in copies:
+        for c in group:
+            c.start()
 
     def rows(first, count):
         return jnp.concatenate([lo_ref[:, first : first + count, :], hi_ref[:, first : first + count, :]], axis=2)
@@ -124,7 +125,7 @@
     d_gate, d_up = [], []
     d_score = jnp.zeros((1, 256), F32)
     for h, (wg, wu, wd) in enumerate(((wg0, wu0, wd0), (wg1, wu1, wd1))):
-        for c in copies[1:] if h else copies[:1]:
+        for c in sum(copies[1:], []) if h else copies[0]:
             c.wait()
         gate = dot(xt, wg[...], (1, 0)).T
         up = dot(xt, wu[...], (1, 0)).T
@@ -158,13 +159,27 @@
     first = iota((WID // 2, 128), 1) < 64
     top = jnp.where(first, parts[0][WID:], parts[1][WID:])
     bottom = jnp.where(first, pltpu.roll(parts[0][WID:], 64, 1), pltpu.roll(parts[1][WID:], 64, 1))
-    whole = jnp.concatenate([parts[0][:WID], parts[1][:WID], jnp.concatenate([top, bottom], axis=0)], axis=1)
-    out_ref[...] = dot(slot_lanes(), whole.astype(BF), (1, 1)).astype(BF)
+    whole = jnp.concatenate([parts[0][:WID], parts[1][:WID], jnp.concatenate([top, bottom], axis=0)], axis=1).astype(BF)
+    src, rank = lane_slots()
+    last = whole[128:]
+    quarters = jnp.concatenate([jnp.where(rank % 4 == i, last, jnp.zeros_like(last)) for i in range(4)], axis=0)
+    row = iota((GRID, SLOTS), 0)
+    heads = (row == src * ROWS + rank).astype(BF)
+    tails = (row == src * ROWS + CAP + rank // 4).astype(BF)
+    out_ref[...] = (dot(heads, whole[:128], (1, 1)) + dot(tails, quarters, (1, 1))).astype(BF)
 
 
 def unpack_kernel(slot_ref, recv_ref, out_ref):
-    place = (iota((GRID, TOK), 0) == slot_ref[...]).astype(BF)
-    out_ref[...] = dot(recv_ref[...], place, (0, 0)).astype(BF)
+    slot, row = slot_ref[...], iota((GRID, TOK), 0)
+    rank = slot % ROWS
+    heads = (row == slot).astype(BF)
+    tails = (row == slot - rank + CAP + rank // 4).astype(BF)
+    out_ref[:128, :] = dot(recv_ref[...], heads, (0, 0)).astype(BF)
+    quarters = dot(recv_ref[...], tails, (0, 0))
+    last = quarters[:32]
+    for i in range(1, 4):
+        last = jnp.where(rank % 4 == i, quarters[32 * i : 32 * (i + 1)], last)
+    out_ref[128:, :] = last.astype(BF)
 
 
 VM = pl.BlockSpec(memory_space=pltpu.VMEM)
@@ -188,29 +203,9 @@
     )
 
 
-def body(tokens, grad_out, expert_ids, router, gate_weight, up_weight, down_weight):
-    me = lax.axis_index("ep").astype(jnp.int32).reshape(1)
-    core = (lax.axis_index("etp") % 2).astype(jnp.int32).reshape(1)
-    other = [(i, i ^ 1) for i in range(N_ETP)]
-    own = [gate_weight[0], up_weight[0], down_weight[0]]
+def expert_call(core, lo, hi, wg1, wu1, wd1, wg, wu, wd):
     shape = jax.ShapeDtypeStruct
-
-    send, slot = call(
-        pack_kernel,
-        [HBM] * 3,
-        [shape((GRID, 2 * WID), BF), shape((1, TOK), jnp.int32)],
-        [VM] * 2,
-        [pltpu.VMEM((1, TOK), jnp.int32), pltpu.VMEM((WID, TOK), BF), pltpu.VMEM((WID, TOK), BF), pltpu.SemaphoreType.DMA((3,))],
-    )(in_hbm(expert_ids.reshape(1, TOK)), in_hbm(tokens.T), in_hbm(grad_out.T))
-    line = call(router_kernel, [SM, VM], shape((8, SLOTS), F32))(me, router.T)
-    recv = lax.all_to_all(send.reshape(EXPERTS, ROWS, 2 * WID), "ep", split_axis=0, concat_axis=0, tiled=True)
-    turned = call(turn_kernel, [VM, VM], shape((AG_ROWS, SLOTS), F32))(recv.reshape(GRID, 2 * WID), line)
-    gathered = lax.all_gather(turned.astype(jnp.float16), "etp", axis=0, tiled=True).reshape(N_ETP, AG_ROWS, SLOTS)
-    lo = lax.dynamic_slice(gathered, (0, 0, 128 * core[0]), (N_ETP, AG_ROWS, 128)).astype(BF)
-    hi = gathered[:, :, 256:].astype(BF)
-    wg, wu, wd = own
-    wg1, wu1, wd1 = (lax.ppermute(w, "etp", other) for w in own)
-    partial = call(
+    return call(
         expert_kernel,
         [SM] + [VM] * 4 + [HBM] * 4,
         shape((N_ETP, WID * 3 // 2, 128), BF),
@@ -221,15 +216,45 @@
             pltpu.VMEM((D, HID), BF),
             pltpu.VMEM((D, HID), BF),
             pltpu.VMEM((HID, D), BF),
-            pltpu.SemaphoreType.DMA((4,)),
+            pltpu.SemaphoreType.DMA((4, 2)),
         ],
         vmem=24 << 20,
         cost=pl.CostEstimate(flops=10 * D * 512 * 256, bytes_accessed=12 << 20, transcendentals=512 * 256),
     )(core, lo, hi, wg1, wu1, *map(in_hbm, (wd1, wg, wu, wd)))
+
+
+def body(tokens, grad_out, expert_ids, router, gate_weight, up_weight, down_weight):
+    me = lax.axis_index("ep").astype(jnp.int32).reshape(1)
+    core = (lax.axis_index("etp") % 2).astype(jnp.int32).reshape(1)
+    other = [(i, i ^ 1) for i in range(N_ETP)]
+    own = [gate_weight[0], up_weight[0], down_weight[0]]
+    shape = jax.ShapeDtypeStruct
+
+    send, slot, line = call(
+        pack_kernel,
+        [SM] + [HBM] * 4,
+        [shape((GRID, 2 * WID), BF), shape((1, TOK), jnp.int32), shape((8, SLOTS), F32)],
+        [VM] * 3,
+        [
+            pltpu.VMEM((1, TOK), jnp.int32),
+            pltpu.VMEM((WID, TOK), BF),
+            pltpu.VMEM((WID, TOK), BF),
+            pltpu.VMEM((EXPERTS, WID), BF),
+            pltpu.SemaphoreType.DMA((4,)),
+        ],
+    )(me, *map(in_hbm, (expert_ids.reshape(1, TOK), tokens.T, grad_out.T, router.T)))
+    recv = lax.all_to_all(send.reshape(EXPERTS, ROWS, 2 * WID), "ep", split_axis=0, concat_axis=0, tiled=True)
+    turned = call(turn_kernel, [VM, VM], shape((AG_ROWS, SLOTS), F32))(recv.reshape(GRID, 2 * WID), line)
+    gathered = lax.all_gather(turned.astype(jnp.float16), "etp", axis=0, tiled=True).reshape(N_ETP, AG_ROWS, SLOTS)
+    lo = lax.dynamic_slice(gathered, (0, 0, 128 * core[0]), (N_ETP, AG_ROWS, 128)).astype(BF)
+    hi = gathered[:, :, 256:].astype(BF)
+    wg, wu, wd = own
+    wg1, wu1, wd1 = (lax.ppermute(w, "etp", other) for w in own)
+    partial = expert_call(core, lo, hi, wg1, wu1, wd1, wg, wu, wd)
     parts = lax.all_to_all(partial, "etp", split_axis=0, concat_axis=0, tiled=True)
-    summed = call(sum_kernel, [VM], shape((GRID, WID), BF))(parts)
-    back = lax.all_to_all(summed.reshape(EXPERTS, ROWS, WID), "ep", split_axis=0, concat_axis=0, tiled=True)
-    out = call(unpack_kernel, [VM] * 2, shape((WID, TOK), BF))(slot, back.reshape(GRID, WID))
+    summed = call(sum_kernel, [VM], shape((GRID, 128), BF))(parts)
+    back = lax.all_to_all(summed.reshape(EXPERTS, ROWS, 128), "ep", split_axis=0, concat_axis=0, tiled=True)
+    out = call(unpack_kernel, [VM] * 2, shape((WID, TOK), BF))(slot, back.reshape(GRID, 128))
     return out.T
 
 

time: 123 us -> 121 us (0.984)
  blocking collectives: 83.5 us -> 81.3 us
    all_to_all x1, blocking collectives: 16.6 us -> 14.3 us  [body(): lax.all_to_all(summed.reshape(EXPERTS, ROWS, 128), 'ep', split_axis=0, co...]
    pallas_call x4 -> x3, Pallas kernels: 10 us -> 9.84 us  [the longest x1 7.19 us: expert_call(): call(expert_kernel, [SM] + [VM] * 4 + [HBM] * 4, shape((N_ETP, WID * 3 //...]
  transfers between devices with their start and end apart: 4 -> 4, of which waited for: 1 -> 1; matrix products, arithmetic and copies ran while one was open for 0% -> 0% of each run, Pallas kernels for 1% -> 0%
where the time goes in v3:
time: 121 us
  blocking collectives  81.3 us (67%)
  starting transfers between devices  20.9 us (17%)
  Pallas kernels  11.2 us (9%)
  waiting for transfers between devices  6.57 us (5%)
    all_gather x1, blocking collectives, body(): lax.all_gather(turned.astype(jnp.float16), 'etp', axis=0, tiled=True)  34.4 us
    all_to_all x1, blocking collectives, body(): lax.all_to_all(partial, 'etp', split_axis=0, concat_axis=0, tiled=True)  32.6 us
    all_to_all x1, blocking collectives, body(): lax.all_to_all(summed.reshape(EXPERTS, ROWS, 128), 'ep', split_axis=0, co...  14.3 us
    all_to_all x1, starting transfers between devices, body(): lax.all_to_all(send.reshape(EXPERTS, ROWS, 2 * WID), 'ep', split_axis=0,...  13.7 us
    ppermute x3, starting transfers between devices, body(): wg1, wu1, wd1 = (lax.ppermute(w, 'etp', other) for w in own)  7.2 us
    pallas_call x1, Pallas kernels, expert_call(): call(expert_kernel, [SM] + [VM] * 4 + [HBM] * 4, shape((N_ETP, WID * 3 //...  7.19 us
    all_to_all x1, waiting for transfers between devices, body(): lax.all_to_all(send.reshape(EXPERTS, ROWS, 2 * WID), 'ep', split_axis=0,...  6.57 us
  transfers between devices with their start and end apart: 4, of which 1 were waited for; matrix products, arithmetic and copies ran while one was open for 0% of the time, Pallas kernels for 0%

profile of v3, /device:TPU:1, one launch (start us, length us, event | category | flops | bytes accessed | tf_op | source)
XLA Modules:
  0.0 120.6 jit_solution(2378325307451365852)
XLA Ops:
  0.0 2.2 %shard_map.73 = (bf16[512,320]{1,0:T(8,128)(2,1)}, s32[1,256]{1,0:T(1,128)S(1)}, f32[8,384]{1,0:T(8,128)S(1)}) custom-call(s32[1]{0:T(128)} %bitcast.me_ref, s32[1,256]{1,0:T(1,128)} %bitcast.22, bf16[160,256]{1,0:T(8,128)(2,1)} %bitcast.19, bf16[160,256]{1,0:T(8,128)(2,1)} %bitcast.20, bf16[32,160]{1,0:T(8,128)(2,1)} %bitcast.21), custom_call_target="tpu_custom_call" | custom-call | tf_op jit(solution)/shard_map/pallas_call | solution.py:233
  2.2 13.7 %all-to-all-start = ((bf16[32,16,320]{2,1,0:T(8,128)(2,1)}), bf16[32,16,320]{2,1,0:T(8,128)(2,1)S(1)}, u32[]{:S(2)}, u32[]{:S(2)}) async-start(bf16[32,16,320]{2,1,0:T(8,128)(2,1)} %bitcast.6), calls=%async_computation | async-start | bytes 786432 | tf_op jit(solution)/shard_map/all_to_all | solution.py:246
  15.9 2.9 %collective-permute-start = (bf16[2560,256]{1,0:T(8,128)(2,1)}, bf16[2560,256]{1,0:T(8,128)(2,1)S(1)}, u32[]{:S(2)}, u32[]{:S(2)}) collective-permute-start(bf16[2560,256]{1,0:T(8,128)(2,1)} %bitcast.23), channel_id=1, source_target_pairs={{0,1},{1,0},{2,3},{3,2},{4,5},{5,4},{6,7},{7,6},{8,9},{9,8},{10,11... | collective-permute-start | bytes 3932168 | tf_op jit(solution)/shard_map/ppermute | solution.py:252
  18.8 1.9 %collective-permute-start.1 = (bf16[2560,256]{1,0:T(8,128)(2,1)}, bf16[2560,256]{1,0:T(8,128)(2,1)S(1)}, u32[]{:S(2)}, u32[]{:S(2)}) collective-permute-start(bf16[2560,256]{1,0:T(8,128)(2,1)} %bitcast.25), channel_id=1, source_target_pairs={{0,1},{1,0},{2,3},{3,2},{4,5},{5,4},{6,7},{7,6},{8,9},{9,8},{10,11... | collective-permute-start | bytes 3932168 | tf_op jit(solution)/shard_map/ppermute | solution.py:252
  20.7 2.4 %collective-permute-start.2 = (bf16[256,2560]{1,0:T(8,128)(2,1)}, bf16[256,2560]{1,0:T(8,128)(2,1)}, u32[]{:S(2)}, u32[]{:S(2)}) collective-permute-start(bf16[256,2560]{1,0:T(8,128)(2,1)} %bitcast.27), channel_id=1, source_target_pairs={{0,1},{1,0},{2,3},{3,2},{4,5},{5,4},{6,7},{7,6},{8,9},{9,8},{10,11... | collective-permute-start | bytes 3932168 | tf_op jit(solution)/shard_map/ppermute | solution.py:252
  23.2 6.6 %all-to-all-done = bf16[32,16,320]{2,1,0:T(8,128)(2,1)S(1)} async-done(((bf16[32,16,320]{2,1,0:T(8,128)(2,1)}), bf16[32,16,320]{2,1,0:T(8,128)(2,1)S(1)}, u32[]{:S(2)}, u32[]{:S(2)}) %all-to-all-start) | async-done | bytes 327712 | tf_op jit(solution)/shard_map/all_to_all | solution.py:246
  29.7 0.4 shard_map.74
  30.2 34.4 %all-gather.1 = f16[5248,384]{1,0:T(8,128)(2,1)S(1)} all-gather(f16[328,384]{1,0:T(8,128)(2,1)S(1)} %convert_element_type.9), channel_id=1, replica_groups=mesh['ep'=32,'etp'=16] {'etp'}, dimensions={0}, use_global_device_ids=true | all-gather | bytes 4282368 | tf_op jit(solution)/shard_map/all_gather | solution.py:248
  64.6 0.5 slice_convert_fusion
  65.1 0.0 collective-permute-done.wg0
  65.1 0.0 collective-permute-done.1.wu0
  65.1 0.0 collective-permute-done.2.wd_other
  65.1 7.2 %shard_map.75 = bf16[16,240,128]{2,1,0:T(8,128)(2,1)S(1)} custom-call(s32[1]{0:T(128)} %bitcast.5.core_ref, bf16[16,328,128]{2,1,0:T(8,128)(2,1)S(1)} %get-tuple-element.12.lo_ref, bf16[16,328,128]{2,1,0:T(8,128)(2,1)S(1)} %get-tuple-element.11.hi_ref, bf16[2560,256]{1,0:T(8,128)(2,1)S(1)} %collective-permute-done.wg0, ...), custom_call_target="tpu_custom_call" | custom-call | flops 3355443200 | bytes 12582912 | tf_op jit(solution)/shard_map/pallas_call | solution.py:208
  72.3 32.6 %all_to_all.15.recv_ref = bf16[16,240,128]{2,1,0:T(8,128)(2,1)S(1)} all-to-all(bf16[16,240,128]{2,1,0:T(8,128)(2,1)S(1)} %shard_map.75), channel_id=1, replica_groups=mesh['ep'=32,'etp'=16] {'etp'}, dimensions={0} | all-to-all | bytes 1966080 | tf_op jit(solution)/shard_map/all_to_all | solution.py:254
  104.9 0.5 shard_map.76
  105.4 14.3 %all_to_all.16 = bf16[32,16,128]{2,1,0:T(8,128)(2,1)S(1)} all-to-all(bf16[32,16,128]{2,1,0:T(8,128)(2,1)S(1)} %bitcast.16), channel_id=1, replica_groups=mesh['ep'=32,'etp'=16] {'ep'}, dimensions={0} | all-to-all | bytes 262144 | tf_op jit(solution)/shard_map/all_to_all | solution.py:256
  119.7 0.9 shard_map.77
  (1 shorter events, 0.0 us)
Async XLA Ops:
  2.2 27.5 %all-to-all-start = ((bf16[32,16,320]{2,1,0:T(8,128)(2,1)}), bf16[32,16,320]{2,1,0:T(8,128)(2,1)S(1)}, u32[]{:S(2)}, u32[]{:S(2)}) async-start(bf16[32,16,320]{2,1,0:T(8,128)(2,1)} %bitcast.6), calls=%async_computation | async-start | bytes 786432 | tf_op jit(solution)/shard_map/all_to_all | solution.py:246
  15.9 49.2 %collective-permute-start = (bf16[2560,256]{1,0:T(8,128)(2,1)}, bf16[2560,256]{1,0:T(8,128)(2,1)S(1)}, u32[]{:S(2)}, u32[]{:S(2)}) collective-permute-start(bf16[2560,256]{1,0:T(8,128)(2,1)} %bitcast.23), channel_id=1, source_target_pairs={{0,1},{1,0},{2,3},{3,2},{4,5},{5,4},{6,7},{7,6},{8,9},{9,8},{10,11... | collective-permute-start | bytes 3932168 | tf_op jit(solution)/shard_map/ppermute | solution.py:252
  18.8 46.3 %collective-permute-start.1 = (bf16[2560,256]{1,0:T(8,128)(2,1)}, bf16[2560,256]{1,0:T(8,128)(2,1)S(1)}, u32[]{:S(2)}, u32[]{:S(2)}) collective-permute-start(bf16[2560,256]{1,0:T(8,128)(2,1)} %bitcast.25), channel_id=1, source_target_pairs={{0,1},{1,0},{2,3},{3,2},{4,5},{5,4},{6,7},{7,6},{8,9},{9,8},{10,11... | collective-permute-start | bytes 3932168 | tf_op jit(solution)/shard_map/ppermute | solution.py:252
  20.7 44.4 %collective-permute-start.2 = (bf16[256,2560]{1,0:T(8,128)(2,1)}, bf16[256,2560]{1,0:T(8,128)(2,1)}, u32[]{:S(2)}, u32[]{:S(2)}) collective-permute-start(bf16[256,2560]{1,0:T(8,128)(2,1)} %bitcast.27), channel_id=1, source_target_pairs={{0,1},{1,0},{2,3},{3,2},{4,5},{5,4},{6,7},{7,6},{8,9},{9,8},{10,11... | collective-permute-start | bytes 3932168 | tf_op jit(solution)/shard_map/ppermute | solution.py:252

commit v4 on v3

--- a/solution.py
+++ b/solution.py
@@ -60,8 +60,8 @@
     ]
     for c in copies:
         c.start()
-    for c in copies:
-        c.wait()
+    copies[0].wait()
+    copies[3].wait()
     mine = (iota((8, EXPERTS), 1) == me_ref[0]).astype(BF)
     column = dot(mine, router_v[...], (1, 0))
     shift = level(jnp.max(jnp.abs(column), axis=1, keepdims=True))
@@ -76,6 +76,8 @@
     slot = ids * ROWS + rank
     slot_ref[...] = slot
     place = (iota((GRID, TOK), 0) == slot).astype(BF)
+    copies[1].wait()
+    copies[2].wait()
     both = jnp.concatenate([x_v[...], g_v[...]], axis=0)
     send_ref[...] = dot(place, both, (1, 1)).astype(BF)
 
@@ -92,41 +94,44 @@
     out_ref[2 * WID :, :] = jnp.where(row < 2, router_ref[...], jnp.where(row == 2, shifts[0], shifts[1]))
 
 
-def expert_kernel(core_ref, lo_ref, hi_ref, wg0, wu0, wd_other, wg_own, wu_own, wd_own, out_ref, x_ref, g_ref, wd0, wg1, wu1, wd1, sems):
+def prepare_kernel(lo_ref, hi_ref, wd_ref, xt_ref, g_ref, score_ref, router_ref, wd_out, x_ref, sems):
+    size = HID // 2
     copies = []
-    for i, (src, dst) in enumerate(((wd_other, wd0), (wg_own, wg1), (wu_own, wu1), (wd_own, wd1))):
-        size = dst.shape[0] // 2
-        parts = [pl.ds(p * size, size) for p in range(2)]
-        copies.append([pltpu.make_async_copy(src.at[at], dst.at[at], sems.at[i, p]) for p, at in enumerate(parts)])
-    for group in copies:
-        for c in group:
-            c.start()
+    for p in range(2):
+        at = pl.ds(p * size, size)
+        copies.append(pltpu.make_async_copy(wd_ref.at[at], wd_out.at[at], sems.at[p]))
+    for c in copies:
+        c.start()
 
     def rows(first, count):
         return jnp.concatenate([lo_ref[:, first : first + count, :], hi_ref[:, first : first + count, :]], axis=2)
 
     extra = rows(2 * WID, 8).astype(F32)
     back = power(-extra)
-    logit = jnp.zeros((1, 256), F32)
-    columns = []
+    lines = jnp.concatenate([extra[j, :1] * back[j, 1:2] for j in range(N_ETP)], axis=0)[:, :WID]
+    columns = lines.T
+    router_ref[...] = columns
+    logit = jnp.zeros((N_ETP, 256), F32)
+    narrow = lines.astype(BF)
     for j in range(N_ETP):
         at = pl.ds(j * WID, WID)
         for first, ref, row in ((0, x_ref, 2), (WID, g_ref, 3)):
             scale = back[j, row : row + 1, :].astype(BF)
             ref[at, :128] = lo_ref[j, first : first + WID, :] * scale[:, :128]
             ref[at, 128:] = hi_ref[j, first : first + WID, :] * scale[:, 128:]
-        line = (extra[j, :8] * back[j, 1:2])[:, :WID]
-        column = line.T[:, :1]
-        logit += jnp.sum(x_ref[at, :].astype(F32) * column, axis=0, keepdims=True)
-        columns.append(column)
-    score = 1.0 / (1.0 + jnp.exp(-logit))
-    xt = x_ref[...].T
-    g = g_ref[...]
+        logit += jnp.where(iota((N_ETP, 256), 0) == j, dot(narrow, x_ref[at, :], (1, 0)), 0.0)
+    logit = jnp.sum(logit, axis=0, keepdims=True)
+    score_ref[...] = 1.0 / (1.0 + jnp.exp(-logit))
+    xt_ref[...] = x_ref[...].T
+    for c in copies:
+        c.wait()
+
+
+def expert_kernel(core_ref, xt_ref, g_ref, score_ref, router_ref, wg0, wu0, wd0, wg1, wu1, wd1, out_ref):
+    score, xt, g = score_ref[...], xt_ref[...], g_ref[...]
     d_gate, d_up = [], []
     d_score = jnp.zeros((1, 256), F32)
-    for h, (wg, wu, wd) in enumerate(((wg0, wu0, wd0), (wg1, wu1, wd1))):
-        for c in sum(copies[1:], []) if h else copies[0]:
-            c.wait()
+    for wg, wu, wd in ((wg0, wu0, wd0), (wg1, wu1, wd1)):
         gate = dot(xt, wg[...], (1, 0)).T
         up = dot(xt, wu[...], (1, 0)).T
         d_hidden = dot(wd[...], g, (1, 0))
@@ -143,7 +148,7 @@
         at = pl.ds(j * WID, WID)
         total = dot(wg0[at, :], d_gate[0], (1, 0)) + dot(wg1[at, :], d_gate[1], (1, 0))
         total += dot(wu0[at, :], d_up[0], (1, 0)) + dot(wu1[at, :], d_up[1], (1, 0))
-        total = total * score + columns[j] * d_logit
+        total = total * score + router_ref[:, j : j + 1] * d_logit
         out_ref[j, :WID, :] = total[:, :128].astype(BF)
         top, bottom = total[: WID // 2, 128:], total[WID // 2 :, 128:]
         out_ref[j, WID:, :] = jnp.where(keep, top, pltpu.roll(bottom, 64, 1)).astype(BF)
@@ -205,22 +210,27 @@
 
 def expert_call(core, lo, hi, wg1, wu1, wd1, wg, wu, wd):
     shape = jax.ShapeDtypeStruct
+    xt, g, score, columns, wd1 = call(
+        prepare_kernel,
+        [VM] * 2 + [HBM],
+        [
+            shape((256, D), BF),
+            shape((D, 256), BF),
+            shape((1, 256), F32),
+            shape((WID, N_ETP), F32),
+            pltpu.VMEM((HID, D), BF),
+        ],
+        [VM] * 5,
+        [pltpu.VMEM((D, 256), BF), pltpu.SemaphoreType.DMA((2,))],
+        vmem=16 << 20,
+    )(lo, hi, in_hbm(wd1))
     return call(
         expert_kernel,
-        [SM] + [VM] * 4 + [HBM] * 4,
+        [SM] + [VM] * 10,
         shape((N_ETP, WID * 3 // 2, 128), BF),
-        scratch=[
-            pltpu.VMEM((D, 256), BF),
-            pltpu.VMEM((D, 256), BF),
-            pltpu.VMEM((HID, D), BF),
-            pltpu.VMEM((D, HID), BF),
-            pltpu.VMEM((D, HID), BF),
-            pltpu.VMEM((HID, D), BF),
-            pltpu.SemaphoreType.DMA((4, 2)),
-        ],
-        vmem=24 << 20,
+        vmem=20 << 20,
         cost=pl.CostEstimate(flops=10 * D * 512 * 256, bytes_accessed=12 << 20, transcendentals=512 * 256),
-    )(core, lo, hi, wg1, wu1, *map(in_hbm, (wd1, wg, wu, wd)))
+    )(core, xt, g, score, columns, wg1, wu1, wd1, wg, wu, wd)
 
 
 def body(tokens, grad_out, expert_ids, router, gate_weight, up_weight, down_weight):

time: 121 us -> 120 us (level)
  Pallas kernels: 11.2 us -> 9.48 us
    pallas_call x1 -> x2, Pallas kernels: 7.19 us -> 5.51 us  [the longest x1 4.06 us: expert_call(): call(expert_kernel, [SM] + [VM] * 10, shape((N_ETP, WID * 3 // 2, 128), B...]
  transfers between devices with their start and end apart: 4 -> 4, of which waited for: 1 -> 1; matrix products, arithmetic and copies ran while one was open for 0% -> 0% of each run, Pallas kernels for 0% -> 2%
where the time goes in v4:
time: 120 us
  blocking collectives  81.2 us (68%)
  starting transfers between devices  20.9 us (17%)
  Pallas kernels  9.48 us (8%)
  waiting for transfers between devices  6.58 us (5%)
    all_gather x1, blocking collectives, body(): lax.all_gather(turned.astype(jnp.float16), 'etp', axis=0, tiled=True)  34.3 us
    all_to_all x1, blocking collectives, body(): lax.all_to_all(partial, 'etp', split_axis=0, concat_axis=0, tiled=True)  32.6 us
    all_to_all x1, blocking collectives, body(): lax.all_to_all(summed.reshape(EXPERTS, ROWS, 128), 'ep', split_axis=0, co...  14.3 us
    all_to_all x1, starting transfers between devices, body(): lax.all_to_all(send.reshape(EXPERTS, ROWS, 2 * WID), 'ep', split_axis=0,...  13.7 us
    ppermute x3, starting transfers between devices, body(): wg1, wu1, wd1 = (lax.ppermute(w, 'etp', other) for w in own)  7.2 us
    all_to_all x1, waiting for transfers between devices, body(): lax.all_to_all(send.reshape(EXPERTS, ROWS, 2 * WID), 'ep', split_axis=0,...  6.57 us
    pallas_call x1, Pallas kernels, expert_call(): call(expert_kernel, [SM] + [VM] * 10, shape((N_ETP, WID * 3 // 2, 128), B...  4.06 us
  transfers between devices with their start and end apart: 4, of which 1 were waited for; matrix products, arithmetic and copies ran while one was open for 0% of the time, Pallas kernels for 2%

profile of v4, /device:TPU:1, one launch (start us, length us, event | category | flops | bytes accessed | tf_op | source)
XLA Modules:
  0.0 119.8 jit_solution(13750615491774966123)
XLA Ops:
  0.0 2.2 %shard_map.73 = (bf16[512,320]{1,0:T(8,128)(2,1)}, s32[1,256]{1,0:T(1,128)S(1)}, f32[8,384]{1,0:T(8,128)S(1)}) custom-call(s32[1]{0:T(128)} %bitcast.me_ref, s32[1,256]{1,0:T(1,128)} %bitcast.28, bf16[160,256]{1,0:T(8,128)(2,1)} %bitcast.25, bf16[160,256]{1,0:T(8,128)(2,1)} %bitcast.26, bf16[32,160]{1,0:T(8,128)(2,1)} %bitcast.27), custom_call_target="tpu_custom_call" | custom-call | tf_op jit(solution)/shard_map/pallas_call | solution.py:243
  2.2 13.7 %all-to-all-start = ((bf16[32,16,320]{2,1,0:T(8,128)(2,1)}), bf16[32,16,320]{2,1,0:T(8,128)(2,1)S(1)}, u32[]{:S(2)}, u32[]{:S(2)}) async-start(bf16[32,16,320]{2,1,0:T(8,128)(2,1)} %bitcast.6), calls=%async_computation | async-start | bytes 786432 | tf_op jit(solution)/shard_map/all_to_all | solution.py:256
  15.9 2.9 %collective-permute-start = (bf16[256,2560]{1,0:T(8,128)(2,1)}, bf16[256,2560]{1,0:T(8,128)(2,1)}, u32[]{:S(2)}, u32[]{:S(2)}) collective-permute-start(bf16[256,2560]{1,0:T(8,128)(2,1)} %bitcast.18), channel_id=1, source_target_pairs={{0,1},{1,0},{2,3},{3,2},{4,5},{5,4},{6,7},{7,6},{8,9},{9,8},{10,11... | collective-permute-start | bytes 3932168 | tf_op jit(solution)/shard_map/ppermute | solution.py:262
  18.8 1.9 %collective-permute-start.1 = (bf16[2560,256]{1,0:T(8,128)(2,1)}, bf16[2560,256]{1,0:T(8,128)(2,1)S(1)}, u32[]{:S(2)}, u32[]{:S(2)}) collective-permute-start(bf16[2560,256]{1,0:T(8,128)(2,1)} %bitcast.20), channel_id=1, source_target_pairs={{0,1},{1,0},{2,3},{3,2},{4,5},{5,4},{6,7},{7,6},{8,9},{9,8},{10,11... | collective-permute-start | bytes 3932168 | tf_op jit(solution)/shard_map/ppermute | solution.py:262
  20.7 2.4 %collective-permute-start.2 = (bf16[2560,256]{1,0:T(8,128)(2,1)}, bf16[2560,256]{1,0:T(8,128)(2,1)S(1)}, u32[]{:S(2)}, u32[]{:S(2)}) collective-permute-start(bf16[2560,256]{1,0:T(8,128)(2,1)} %bitcast.22), channel_id=1, source_target_pairs={{0,1},{1,0},{2,3},{3,2},{4,5},{5,4},{6,7},{7,6},{8,9},{9,8},{10,11... | collective-permute-start | bytes 3932168 | tf_op jit(solution)/shard_map/ppermute | solution.py:262
  23.2 6.6 %all-to-all-done = bf16[32,16,320]{2,1,0:T(8,128)(2,1)S(1)} async-done(((bf16[32,16,320]{2,1,0:T(8,128)(2,1)}), bf16[32,16,320]{2,1,0:T(8,128)(2,1)S(1)}, u32[]{:S(2)}, u32[]{:S(2)}) %all-to-all-start) | async-done | bytes 327712 | tf_op jit(solution)/shard_map/all_to_all | solution.py:256
  29.7 0.4 shard_map.74
  30.2 34.3 %all-gather.1 = f16[5248,384]{1,0:T(8,128)(2,1)S(1)} all-gather(f16[328,384]{1,0:T(8,128)(2,1)S(1)} %convert_element_type.9), channel_id=1, replica_groups=mesh['ep'=32,'etp'=16] {'etp'}, dimensions={0}, use_global_device_ids=true | all-gather | bytes 4282368 | tf_op jit(solution)/shard_map/all_gather | solution.py:258
  64.5 0.5 slice_convert_fusion
  65.0 0.0 collective-permute-done.wd_ref
  65.0 0.0 copy-start
  65.0 0.0 copy-start.1
  65.0 0.0 copy-start.2
  65.0 1.5 %shard_map.75 = (bf16[256,2560]{1,0:T(8,128)(2,1)S(1)}, bf16[2560,256]{1,0:T(8,128)(2,1)S(1)}, f32[1,256]{1,0:T(1,128)S(1)}, f32[160,16]{1,0:T(8,128)S(1)}, bf16[256,2560]{1,0:T(8,128)(2,1)S(1)}) custom-call(bf16[16,328,128]{2,1,0:T(8,128)(2,1)S(1)} %get-tuple-element.22.lo_ref, bf16[16,328,128]{2,1,0:T(8,128)(2,1)S(1)} %get-tuple-element.21.hi_ref, ...), custom_call_target="tpu_custom_call" | custom-call | tf_op jit(solution)/shard_map/pallas_call | solution.py:213
  66.5 0.0 collective-permute-done.1.wg0
  66.5 0.0 collective-permute-done.2.wu0
  66.5 0.2 copy-done
  66.7 0.4 copy-done.1
  67.1 0.4 copy-done.2
  67.5 4.1 %shard_map.76 = bf16[16,240,128]{2,1,0:T(8,128)(2,1)S(1)} custom-call(s32[1]{0:T(128)} %bitcast.5.core_ref, bf16[256,2560]{1,0:T(8,128)(2,1)S(1)} %get-tuple-element.16.xt_ref, bf16[2560,256]{1,0:T(8,128)(2,1)S(1)} %get-tuple-element.17.g_ref, f32[1,256]{1,0:T(1,128)S(1)} %get-tuple-element.18.score_ref, f32[160,16]{1,0:T(8,128)S(1)} %get-tuple-element.19.router_ref, ...), custom_call_target="tpu_custom_call" | custom-call | flops 3355443200 | bytes 12582912 | tf_op jit(solution)/shard_map/pallas_call | solution.py:227
  71.6 32.6 %all_to_all.15.recv_ref = bf16[16,240,128]{2,1,0:T(8,128)(2,1)S(1)} all-to-all(bf16[16,240,128]{2,1,0:T(8,128)(2,1)S(1)} %shard_map.76), channel_id=1, replica_groups=mesh['ep'=32,'etp'=16] {'etp'}, dimensions={0} | all-to-all | bytes 1966080 | tf_op jit(solution)/shard_map/all_to_all | solution.py:264
  104.2 0.5 shard_map.77
  104.6 14.3 %all_to_all.16 = bf16[32,16,128]{2,1,0:T(8,128)(2,1)S(1)} all-to-all(bf16[32,16,128]{2,1,0:T(8,128)(2,1)S(1)} %bitcast.16), channel_id=1, replica_groups=mesh['ep'=32,'etp'=16] {'ep'}, dimensions={0} | all-to-all | bytes 262144 | tf_op jit(solution)/shard_map/all_to_all | solution.py:266
  118.9 0.9 shard_map.78
  (1 shorter events, 0.0 us)
Async XLA Ops:
  2.2 27.5 %all-to-all-start = ((bf16[32,16,320]{2,1,0:T(8,128)(2,1)}), bf16[32,16,320]{2,1,0:T(8,128)(2,1)S(1)}, u32[]{:S(2)}, u32[]{:S(2)}) async-start(bf16[32,16,320]{2,1,0:T(8,128)(2,1)} %bitcast.6), calls=%async_computation | async-start | bytes 786432 | tf_op jit(solution)/shard_map/all_to_all | solution.py:256
  15.9 49.1 %collective-permute-start = (bf16[256,2560]{1,0:T(8,128)(2,1)}, bf16[256,2560]{1,0:T(8,128)(2,1)}, u32[]{:S(2)}, u32[]{:S(2)}) collective-permute-start(bf16[256,2560]{1,0:T(8,128)(2,1)} %bitcast.18), channel_id=1, source_target_pairs={{0,1},{1,0},{2,3},{3,2},{4,5},{5,4},{6,7},{7,6},{8,9},{9,8},{10,11... | collective-permute-start | bytes 3932168 | tf_op jit(solution)/shard_map/ppermute | solution.py:262
  18.8 47.7 %collective-permute-start.1 = (bf16[2560,256]{1,0:T(8,128)(2,1)}, bf16[2560,256]{1,0:T(8,128)(2,1)S(1)}, u32[]{:S(2)}, u32[]{:S(2)}) collective-permute-start(bf16[2560,256]{1,0:T(8,128)(2,1)} %bitcast.20), channel_id=1, source_target_pairs={{0,1},{1,0},{2,3},{3,2},{4,5},{5,4},{6,7},{7,6},{8,9},{9,8},{10,11... | collective-permute-start | bytes 3932168 | tf_op jit(solution)/shard_map/ppermute | solution.py:262
  20.7 45.8 %collective-permute-start.2 = (bf16[2560,256]{1,0:T(8,128)(2,1)}, bf16[2560,256]{1,0:T(8,128)(2,1)S(1)}, u32[]{:S(2)}, u32[]{:S(2)}) collective-permute-start(bf16[2560,256]{1,0:T(8,128)(2,1)} %bitcast.22), channel_id=1, source_target_pairs={{0,1},{1,0},{2,3},{3,2},{4,5},{5,4},{6,7},{7,6},{8,9},{9,8},{10,11... | collective-permute-start | bytes 3932168 | tf_op jit(solution)/shard_map/ppermute | solution.py:262
  65.0 1.7 %copy-start = (bf16[1,256,2560]{2,1,0:T(8,128)(2,1)S(1)}, bf16[1,256,2560]{2,1,0:T(8,128)(2,1)}, u32[]{:S(2)}) copy-start(bf16[1,256,2560]{2,1,0:T(8,128)(2,1)} %param.13) | copy-start | bytes 3932164
  65.0 2.1 %copy-start.1 = (bf16[1,2560,256]{2,1,0:T(8,128)(2,1)S(1)}, bf16[1,2560,256]{2,1,0:T(8,128)(2,1)}, u32[]{:S(2)}) copy-start(bf16[1,2560,256]{2,1,0:T(8,128)(2,1)} %param.11) | copy-start | bytes 3932164
  65.0 2.5 %copy-start.2 = (bf16[1,2560,256]{2,1,0:T(8,128)(2,1)S(1)}, bf16[1,2560,256]{2,1,0:T(8,128)(2,1)}, u32[]{:S(2)}) copy-start(bf16[1,2560,256]{2,1,0:T(8,128)(2,1)} %param.12) | copy-start | bytes 3932164

commit v5 on v4

--- a/solution.py
+++ b/solution.py
@@ -19,6 +19,16 @@
 AG_ROWS = 2 * WID + 8
 F32 = jnp.float32
 BF = jnp.bfloat16
+
+
+ETP_ORDER = [2 * y + y % 2 for y in range(8)] + [2 * y + 1 - y % 2 for y in range(7, -1, -1)]
+ETP_PLACE = [ETP_ORDER.index(i) for i in range(N_ETP)]
+EP_ORDER = [4 * z + (x + z) % 4 for x in range(4) for z in range(8)]
+
+
+def ep_place(i):
+    z = i // 4
+    return (i - z) % 4 * 8 + z
 
 
 def iota(shape, dim):
@@ -73,7 +83,7 @@
     before = (iota((TOK, TOK), 0) < iota((TOK, TOK), 1)).astype(BF)
     earlier = dot(picked.astype(BF), before, (1, 0))
     rank = jnp.sum(jnp.where(picked, earlier, 0.0), axis=0, keepdims=True).astype(jnp.int32)
-    slot = ids * ROWS + rank
+    slot = ep_place(ids) * ROWS + rank
     slot_ref[...] = slot
     place = (iota((GRID, TOK), 0) == slot).astype(BF)
     copies[1].wait()
@@ -149,17 +159,17 @@
         total = dot(wg0[at, :], d_gate[0], (1, 0)) + dot(wg1[at, :], d_gate[1], (1, 0))
         total += dot(wu0[at, :], d_up[0], (1, 0)) + dot(wu1[at, :], d_up[1], (1, 0))
         total = total * score + router_ref[:, j : j + 1] * d_logit
-        out_ref[j, :WID, :] = total[:, :128].astype(BF)
+        out_ref[ETP_PLACE[j], :WID, :] = total[:, :128].astype(BF)
         top, bottom = total[: WID // 2, 128:], total[WID // 2 :, 128:]
-        out_ref[j, WID:, :] = jnp.where(keep, top, pltpu.roll(bottom, 64, 1)).astype(BF)
+        out_ref[ETP_PLACE[j], WID:, :] = jnp.where(keep, top, pltpu.roll(bottom, 64, 1)).astype(BF)
 
 
 def sum_kernel(recv_ref, out_ref):
     parts = []
     for c in range(2):
-        total = recv_ref[c].astype(F32)
+        total = recv_ref[ETP_PLACE[c]].astype(F32)
         for y in range(1, N_ETP // 2):
-            total += recv_ref[2 * y + c].astype(F32)
+            total += recv_ref[ETP_PLACE[2 * y + c]].astype(F32)
         parts.append(total)
     first = iota((WID // 2, 128), 1) < 64
     top = jnp.where(first, parts[0][WID:], parts[1][WID:])
@@ -253,7 +263,7 @@
             pltpu.SemaphoreType.DMA((4,)),
         ],
     )(me, *map(in_hbm, (expert_ids.reshape(1, TOK), tokens.T, grad_out.T, router.T)))
-    recv = lax.all_to_all(send.reshape(EXPERTS, ROWS, 2 * WID), "ep", split_axis=0, concat_axis=0, tiled=True)
+    recv = lax.all_to_all(send.reshape(EXPERTS, ROWS, 2 * WID), "ep", split_axis=0, concat_axis=0, tiled=True, axis_index_groups=[EP_ORDER])
     turned = call(turn_kernel, [VM, VM], shape((AG_ROWS, SLOTS), F32))(recv.reshape(GRID, 2 * WID), line)
     gathered = lax.all_gather(turned.astype(jnp.float16), "etp", axis=0, tiled=True).reshape(N_ETP, AG_ROWS, SLOTS)
     lo = lax.dynamic_slice(gathered, (0, 0, 128 * core[0]), (N_ETP, AG_ROWS, 128)).astype(BF)
@@ -261,9 +271,9 @@
     wg, wu, wd = own
     wg1, wu1, wd1 = (lax.ppermute(w, "etp", other) for w in own)
     partial = expert_call(core, lo, hi, wg1, wu1, wd1, wg, wu, wd)
-    parts = lax.all_to_all(partial, "etp", split_axis=0, concat_axis=0, tiled=True)
+    parts = lax.all_to_all(partial, "etp", split_axis=0, concat_axis=0, tiled=True, axis_index_groups=[ETP_ORDER])
     summed = call(sum_kernel, [VM], shape((GRID, 128), BF))(parts)
-    back = lax.all_to_all(summed.reshape(EXPERTS, ROWS, 128), "ep", split_axis=0, concat_axis=0, tiled=True)
+    back = lax.all_to_all(summed.reshape(EXPERTS, ROWS, 128), "ep", split_axis=0, concat_axis=0, tiled=True, axis_index_groups=[EP_ORDER])
     out = call(unpack_kernel, [VM] * 2, shape((WID, TOK), BF))(slot, back.reshape(GRID, 128))
     return out.T
 

time: 120 us -> 119 us (level)
  waiting for transfers between devices: 6.58 us -> 5.05 us
    all_to_all x1, waiting for transfers between devices: 6.57 us -> 5.05 us  [body(): lax.all_to_all(send.reshape(EXPERTS, ROWS, 2 * WID), 'ep', split_axis=0,...]
where the time goes in v5:
time: 119 us; the launch traced here: 118 us
  blocking collectives  81.4 us (68%)
  starting transfers between devices  20.9 us (18%)
  Pallas kernels  9.47 us (8%)
  waiting for transfers between devices  5.05 us (4%)
    all_gather x1, blocking collectives, body(): lax.all_gather(turned.astype(jnp.float16), 'etp', axis=0, tiled=True)  35 us
    all_to_all x1, blocking collectives, body(): lax.all_to_all(partial, 'etp', split_axis=0, concat_axis=0, tiled=True, a...  32.6 us
    all_to_all x1, blocking collectives, body(): lax.all_to_all(summed.reshape(EXPERTS, ROWS, 128), 'ep', split_axis=0, co...  13.8 us
    all_to_all x1, starting transfers between devices, body(): lax.all_to_all(send.reshape(EXPERTS, ROWS, 2 * WID), 'ep', split_axis=0,...  13.7 us
    ppermute x3, starting transfers between devices, body(): wg1, wu1, wd1 = (lax.ppermute(w, 'etp', other) for w in own)  7.2 us
    all_to_all x1, waiting for transfers between devices, body(): lax.all_to_all(send.reshape(EXPERTS, ROWS, 2 * WID), 'ep', split_axis=0,...  5.05 us
    pallas_call x1, Pallas kernels, expert_call(): call(expert_kernel, [SM] + [VM] * 10, shape((N_ETP, WID * 3 // 2, 128), B...  4.06 us
  transfers between devices with their start and end apart: 4, of which 1 were waited for; matrix products, arithmetic and copies ran while one was open for 0% of the time, Pallas kernels for 2%

profile of v5, /device:TPU:1, one launch (start us, length us, event | category | flops | bytes accessed | tf_op | source)
XLA Modules:
  0.0 118.5 jit_solution(3574270316897111013)
XLA Ops:
  0.0 2.2 %shard_map.73 = (bf16[512,320]{1,0:T(8,128)(2,1)}, s32[1,256]{1,0:T(1,128)S(1)}, f32[8,384]{1,0:T(8,128)S(1)}) custom-call(s32[1]{0:T(128)} %bitcast.me_ref, s32[1,256]{1,0:T(1,128)} %bitcast.28, bf16[160,256]{1,0:T(8,128)(2,1)} %bitcast.25, bf16[160,256]{1,0:T(8,128)(2,1)} %bitcast.26, bf16[32,160]{1,0:T(8,128)(2,1)} %bitcast.27), custom_call_target="tpu_custom_call" | custom-call | tf_op jit(solution)/shard_map/pallas_call | solution.py:253
  2.2 13.7 %all-to-all-start = ((bf16[32,16,320]{2,1,0:T(8,128)(2,1)}), bf16[32,16,320]{2,1,0:T(8,128)(2,1)S(1)}, u32[]{:S(2)}, u32[]{:S(2)}) async-start(bf16[32,16,320]{2,1,0:T(8,128)(2,1)} %bitcast.6), calls=%async_computation | async-start | bytes 786432 | tf_op jit(solution)/shard_map/all_to_all | solution.py:266
  15.9 2.9 %collective-permute-start = (bf16[256,2560]{1,0:T(8,128)(2,1)}, bf16[256,2560]{1,0:T(8,128)(2,1)}, u32[]{:S(2)}, u32[]{:S(2)}) collective-permute-start(bf16[256,2560]{1,0:T(8,128)(2,1)} %bitcast.18), channel_id=1, source_target_pairs={{0,1},{1,0},{2,3},{3,2},{4,5},{5,4},{6,7},{7,6},{8,9},{9,8},{10,11... | collective-permute-start | bytes 3932168 | tf_op jit(solution)/shard_map/ppermute | solution.py:272
  18.8 1.9 %collective-permute-start.1 = (bf16[2560,256]{1,0:T(8,128)(2,1)}, bf16[2560,256]{1,0:T(8,128)(2,1)S(1)}, u32[]{:S(2)}, u32[]{:S(2)}) collective-permute-start(bf16[2560,256]{1,0:T(8,128)(2,1)} %bitcast.20), channel_id=1, source_target_pairs={{0,1},{1,0},{2,3},{3,2},{4,5},{5,4},{6,7},{7,6},{8,9},{9,8},{10,11... | collective-permute-start | bytes 3932168 | tf_op jit(solution)/shard_map/ppermute | solution.py:272
  20.7 2.4 %collective-permute-start.2 = (bf16[2560,256]{1,0:T(8,128)(2,1)}, bf16[2560,256]{1,0:T(8,128)(2,1)S(1)}, u32[]{:S(2)}, u32[]{:S(2)}) collective-permute-start(bf16[2560,256]{1,0:T(8,128)(2,1)} %bitcast.22), channel_id=1, source_target_pairs={{0,1},{1,0},{2,3},{3,2},{4,5},{5,4},{6,7},{7,6},{8,9},{9,8},{10,11... | collective-permute-start | bytes 3932168 | tf_op jit(solution)/shard_map/ppermute | solution.py:272
  23.2 5.0 %all-to-all-done = bf16[32,16,320]{2,1,0:T(8,128)(2,1)S(1)} async-done(((bf16[32,16,320]{2,1,0:T(8,128)(2,1)}), bf16[32,16,320]{2,1,0:T(8,128)(2,1)S(1)}, u32[]{:S(2)}, u32[]{:S(2)}) %all-to-all-start) | async-done | bytes 327712 | tf_op jit(solution)/shard_map/all_to_all | solution.py:266
  28.2 0.4 shard_map.74
  28.7 35.0 %all-gather.1 = f16[5248,384]{1,0:T(8,128)(2,1)S(1)} all-gather(f16[328,384]{1,0:T(8,128)(2,1)S(1)} %convert_element_type.9), channel_id=1, replica_groups=mesh['ep'=32,'etp'=16] {'etp'}, dimensions={0}, use_global_device_ids=true | all-gather | bytes 4282368 | tf_op jit(solution)/shard_map/all_gather | solution.py:268
  63.7 0.5 slice_convert_fusion
  64.2 0.0 collective-permute-done.wd_ref
  64.2 0.0 copy-start
  64.2 0.0 copy-start.1
  64.2 0.0 copy-start.2
  64.2 1.5 %shard_map.75 = (bf16[256,2560]{1,0:T(8,128)(2,1)S(1)}, bf16[2560,256]{1,0:T(8,128)(2,1)S(1)}, f32[1,256]{1,0:T(1,128)S(1)}, f32[160,16]{1,0:T(8,128)S(1)}, bf16[256,2560]{1,0:T(8,128)(2,1)S(1)}) custom-call(bf16[16,328,128]{2,1,0:T(8,128)(2,1)S(1)} %get-tuple-element.22.lo_ref, bf16[16,328,128]{2,1,0:T(8,128)(2,1)S(1)} %get-tuple-element.21.hi_ref, ...), custom_call_target="tpu_custom_call" | custom-call | tf_op jit(solution)/shard_map/pallas_call | solution.py:223
  65.7 0.0 collective-permute-done.1.wg0
  65.7 0.0 collective-permute-done.2.wu0
  65.7 0.2 copy-done
  65.9 0.4 copy-done.1
  66.3 0.4 copy-done.2
  66.7 4.1 %shard_map.76 = bf16[16,240,128]{2,1,0:T(8,128)(2,1)S(1)} custom-call(s32[1]{0:T(128)} %bitcast.5.core_ref, bf16[256,2560]{1,0:T(8,128)(2,1)S(1)} %get-tuple-element.16.xt_ref, bf16[2560,256]{1,0:T(8,128)(2,1)S(1)} %get-tuple-element.17.g_ref, f32[1,256]{1,0:T(1,128)S(1)} %get-tuple-element.18.score_ref, f32[160,16]{1,0:T(8,128)S(1)} %get-tuple-element.19.router_ref, ...), custom_call_target="tpu_custom_call" | custom-call | flops 3355443200 | bytes 12582912 | tf_op jit(solution)/shard_map/pallas_call | solution.py:237
  70.8 32.6 %all_to_all.15.recv_ref = bf16[16,240,128]{2,1,0:T(8,128)(2,1)S(1)} all-to-all(bf16[16,240,128]{2,1,0:T(8,128)(2,1)S(1)} %shard_map.76), channel_id=1, replica_groups={{0,3,4,7,8,11,12,15,14,13,10,9,6,5,2,1},{16,19,20,23,24,27,28,31,30,29,..., dimensions={0} | all-to-all | bytes 1966080 | tf_op jit(solution)/shard_map/all_to_all | solution.py:274
  103.4 0.5 shard_map.77
  103.8 13.8 %all_to_all.16 = bf16[32,16,128]{2,1,0:T(8,128)(2,1)S(1)} all-to-all(bf16[32,16,128]{2,1,0:T(8,128)(2,1)S(1)} %bitcast.16), channel_id=1, replica_groups={{0,80,160,240,256,336,416,496,16,96,176,192,272,352,432,448,32,112,128,..., dimensions={0} | all-to-all | bytes 262144 | tf_op jit(solution)/shard_map/all_to_all | solution.py:276
  117.6 0.9 shard_map.78
  (1 shorter events, 0.0 us)
Async XLA Ops:
  2.2 26.0 %all-to-all-start = ((bf16[32,16,320]{2,1,0:T(8,128)(2,1)}), bf16[32,16,320]{2,1,0:T(8,128)(2,1)S(1)}, u32[]{:S(2)}, u32[]{:S(2)}) async-start(bf16[32,16,320]{2,1,0:T(8,128)(2,1)} %bitcast.6), calls=%async_computation | async-start | bytes 786432 | tf_op jit(solution)/shard_map/all_to_all | solution.py:266
  15.9 48.3 %collective-permute-start = (bf16[256,2560]{1,0:T(8,128)(2,1)}, bf16[256,2560]{1,0:T(8,128)(2,1)}, u32[]{:S(2)}, u32[]{:S(2)}) collective-permute-start(bf16[256,2560]{1,0:T(8,128)(2,1)} %bitcast.18), channel_id=1, source_target_pairs={{0,1},{1,0},{2,3},{3,2},{4,5},{5,4},{6,7},{7,6},{8,9},{9,8},{10,11... | collective-permute-start | bytes 3932168 | tf_op jit(solution)/shard_map/ppermute | solution.py:272
  18.8 46.9 %collective-permute-start.1 = (bf16[2560,256]{1,0:T(8,128)(2,1)}, bf16[2560,256]{1,0:T(8,128)(2,1)S(1)}, u32[]{:S(2)}, u32[]{:S(2)}) collective-permute-start(bf16[2560,256]{1,0:T(8,128)(2,1)} %bitcast.20), channel_id=1, source_target_pairs={{0,1},{1,0},{2,3},{3,2},{4,5},{5,4},{6,7},{7,6},{8,9},{9,8},{10,11... | collective-permute-start | bytes 3932168 | tf_op jit(solution)/shard_map/ppermute | solution.py:272
  20.7 45.0 %collective-permute-start.2 = (bf16[2560,256]{1,0:T(8,128)(2,1)}, bf16[2560,256]{1,0:T(8,128)(2,1)S(1)}, u32[]{:S(2)}, u32[]{:S(2)}) collective-permute-start(bf16[2560,256]{1,0:T(8,128)(2,1)} %bitcast.22), channel_id=1, source_target_pairs={{0,1},{1,0},{2,3},{3,2},{4,5},{5,4},{6,7},{7,6},{8,9},{9,8},{10,11... | collective-permute-start | bytes 3932168 | tf_op jit(solution)/shard_map/ppermute | solution.py:272
  64.2 1.7 %copy-start = (bf16[1,256,2560]{2,1,0:T(8,128)(2,1)S(1)}, bf16[1,256,2560]{2,1,0:T(8,128)(2,1)}, u32[]{:S(2)}) copy-start(bf16[1,256,2560]{2,1,0:T(8,128)(2,1)} %param.13) | copy-start | bytes 3932164
  64.2 2.1 %copy-start.1 = (bf16[1,2560,256]{2,1,0:T(8,128)(2,1)S(1)}, bf16[1,2560,256]{2,1,0:T(8,128)(2,1)}, u32[]{:S(2)}) copy-start(bf16[1,2560,256]{2,1,0:T(8,128)(2,1)} %param.11) | copy-start | bytes 3932164
  64.2 2.5 %copy-start.2 = (bf16[1,2560,256]{2,1,0:T(8,128)(2,1)S(1)}, bf16[1,2560,256]{2,1,0:T(8,128)(2,1)}, u32[]{:S(2)}) copy-start(bf16[1,2560,256]{2,1,0:T(8,128)(2,1)} %param.12) | copy-start | bytes 3932164

commit v6 on v5

--- a/solution.py
+++ b/solution.py
@@ -21,7 +21,7 @@
 BF = jnp.bfloat16
 
 
-ETP_ORDER = [2 * y + y % 2 for y in range(8)] + [2 * y + 1 - y % 2 for y in range(7, -1, -1)]
+ETP_ORDER = [2 * y + y % 2 for y in range(8)] + [2 * y + 1 - y % 2 for y in range(8)]
 ETP_PLACE = [ETP_ORDER.index(i) for i in range(N_ETP)]
 EP_ORDER = [4 * z + (x + z) % 4 for x in range(4) for z in range(8)]
 

time: 119 us -> 118 us (level)
  blocking collectives: 81.4 us -> 80.1 us
    all_to_all x1, blocking collectives: 32.6 us -> 30.5 us  [body(): lax.all_to_all(partial, 'etp', split_axis=0, concat_axis=0, tiled=True, a...]
where the time goes in v6:
time: 118 us; the launch traced here: 117 us
  blocking collectives  80.1 us (68%)
  starting transfers between devices  20.9 us (18%)
  Pallas kernels  9.47 us (8%)
  waiting for transfers between devices  5.05 us (4%)
    all_gather x1, blocking collectives, body(): lax.all_gather(turned.astype(jnp.float16), 'etp', axis=0, tiled=True)  35 us
    all_to_all x1, blocking collectives, body(): lax.all_to_all(partial, 'etp', split_axis=0, concat_axis=0, tiled=True, a...  30.5 us
    all_to_all x1, blocking collectives, body(): lax.all_to_all(summed.reshape(EXPERTS, ROWS, 128), 'ep', split_axis=0, co...  14.6 us
    all_to_all x1, starting transfers between devices, body(): lax.all_to_all(send.reshape(EXPERTS, ROWS, 2 * WID), 'ep', split_axis=0,...  13.7 us
    ppermute x3, starting transfers between devices, body(): wg1, wu1, wd1 = (lax.ppermute(w, 'etp', other) for w in own)  7.2 us
    all_to_all x1, waiting for transfers between devices, body(): lax.all_to_all(send.reshape(EXPERTS, ROWS, 2 * WID), 'ep', split_axis=0,...  5.05 us
    pallas_call x1, Pallas kernels, expert_call(): call(expert_kernel, [SM] + [VM] * 10, shape((N_ETP, WID * 3 // 2, 128), B...  4.06 us
  transfers between devices with their start and end apart: 4, of which 1 were waited for; matrix products, arithmetic and copies ran while one was open for 0% of the time, Pallas kernels for 2%

profile of v6, /device:TPU:1, one launch (start us, length us, event | category | flops | bytes accessed | tf_op | source)
XLA Modules:
  0.0 117.2 jit_solution(2735010819998885193)
XLA Ops:
  0.0 2.2 %shard_map.73 = (bf16[512,320]{1,0:T(8,128)(2,1)}, s32[1,256]{1,0:T(1,128)S(1)}, f32[8,384]{1,0:T(8,128)S(1)}) custom-call(s32[1]{0:T(128)} %bitcast.me_ref, s32[1,256]{1,0:T(1,128)} %bitcast.28, bf16[160,256]{1,0:T(8,128)(2,1)} %bitcast.25, bf16[160,256]{1,0:T(8,128)(2,1)} %bitcast.26, bf16[32,160]{1,0:T(8,128)(2,1)} %bitcast.27), custom_call_target="tpu_custom_call" | custom-call | tf_op jit(solution)/shard_map/pallas_call | solution.py:253
  2.2 13.7 %all-to-all-start = ((bf16[32,16,320]{2,1,0:T(8,128)(2,1)}), bf16[32,16,320]{2,1,0:T(8,128)(2,1)S(1)}, u32[]{:S(2)}, u32[]{:S(2)}) async-start(bf16[32,16,320]{2,1,0:T(8,128)(2,1)} %bitcast.6), calls=%async_computation | async-start | bytes 786432 | tf_op jit(solution)/shard_map/all_to_all | solution.py:266
  15.9 2.9 %collective-permute-start = (bf16[256,2560]{1,0:T(8,128)(2,1)}, bf16[256,2560]{1,0:T(8,128)(2,1)}, u32[]{:S(2)}, u32[]{:S(2)}) collective-permute-start(bf16[256,2560]{1,0:T(8,128)(2,1)} %bitcast.18), channel_id=1, source_target_pairs={{0,1},{1,0},{2,3},{3,2},{4,5},{5,4},{6,7},{7,6},{8,9},{9,8},{10,11... | collective-permute-start | bytes 3932168 | tf_op jit(solution)/shard_map/ppermute | solution.py:272
  18.8 1.9 %collective-permute-start.1 = (bf16[2560,256]{1,0:T(8,128)(2,1)}, bf16[2560,256]{1,0:T(8,128)(2,1)S(1)}, u32[]{:S(2)}, u32[]{:S(2)}) collective-permute-start(bf16[2560,256]{1,0:T(8,128)(2,1)} %bitcast.20), channel_id=1, source_target_pairs={{0,1},{1,0},{2,3},{3,2},{4,5},{5,4},{6,7},{7,6},{8,9},{9,8},{10,11... | collective-permute-start | bytes 3932168 | tf_op jit(solution)/shard_map/ppermute | solution.py:272
  20.7 2.4 %collective-permute-start.2 = (bf16[2560,256]{1,0:T(8,128)(2,1)}, bf16[2560,256]{1,0:T(8,128)(2,1)S(1)}, u32[]{:S(2)}, u32[]{:S(2)}) collective-permute-start(bf16[2560,256]{1,0:T(8,128)(2,1)} %bitcast.22), channel_id=1, source_target_pairs={{0,1},{1,0},{2,3},{3,2},{4,5},{5,4},{6,7},{7,6},{8,9},{9,8},{10,11... | collective-permute-start | bytes 3932168 | tf_op jit(solution)/shard_map/ppermute | solution.py:272
  23.2 5.0 %all-to-all-done = bf16[32,16,320]{2,1,0:T(8,128)(2,1)S(1)} async-done(((bf16[32,16,320]{2,1,0:T(8,128)(2,1)}), bf16[32,16,320]{2,1,0:T(8,128)(2,1)S(1)}, u32[]{:S(2)}, u32[]{:S(2)}) %all-to-all-start) | async-done | bytes 327712 | tf_op jit(solution)/shard_map/all_to_all | solution.py:266
  28.2 0.4 shard_map.74
  28.7 35.0 %all-gather.1 = f16[5248,384]{1,0:T(8,128)(2,1)S(1)} all-gather(f16[328,384]{1,0:T(8,128)(2,1)S(1)} %convert_element_type.9), channel_id=1, replica_groups=mesh['ep'=32,'etp'=16] {'etp'}, dimensions={0}, use_global_device_ids=true | all-gather | bytes 4282368 | tf_op jit(solution)/shard_map/all_gather | solution.py:268
  63.7 0.5 slice_convert_fusion
  64.2 0.0 collective-permute-done.wd_ref
  64.2 0.0 copy-start
  64.2 0.0 copy-start.1
  64.2 0.0 copy-start.2
  64.2 1.5 %shard_map.75 = (bf16[256,2560]{1,0:T(8,128)(2,1)S(1)}, bf16[2560,256]{1,0:T(8,128)(2,1)S(1)}, f32[1,256]{1,0:T(1,128)S(1)}, f32[160,16]{1,0:T(8,128)S(1)}, bf16[256,2560]{1,0:T(8,128)(2,1)S(1)}) custom-call(bf16[16,328,128]{2,1,0:T(8,128)(2,1)S(1)} %get-tuple-element.22.lo_ref, bf16[16,328,128]{2,1,0:T(8,128)(2,1)S(1)} %get-tuple-element.21.hi_ref, ...), custom_call_target="tpu_custom_call" | custom-call | tf_op jit(solution)/shard_map/pallas_call | solution.py:223
  65.7 0.0 collective-permute-done.1.wg0
  65.7 0.0 collective-permute-done.2.wu0
  65.7 0.2 copy-done
  65.9 0.4 copy-done.1
  66.3 0.4 copy-done.2
  66.7 4.1 %shard_map.76 = bf16[16,240,128]{2,1,0:T(8,128)(2,1)S(1)} custom-call(s32[1]{0:T(128)} %bitcast.5.core_ref, bf16[256,2560]{1,0:T(8,128)(2,1)S(1)} %get-tuple-element.16.xt_ref, bf16[2560,256]{1,0:T(8,128)(2,1)S(1)} %get-tuple-element.17.g_ref, f32[1,256]{1,0:T(1,128)S(1)} %get-tuple-element.18.score_ref, f32[160,16]{1,0:T(8,128)S(1)} %get-tuple-element.19.router_ref, ...), custom_call_target="tpu_custom_call" | custom-call | flops 3355443200 | bytes 12582912 | tf_op jit(solution)/shard_map/pallas_call | solution.py:237
  70.8 30.5 %all_to_all.15.recv_ref = bf16[16,240,128]{2,1,0:T(8,128)(2,1)S(1)} all-to-all(bf16[16,240,128]{2,1,0:T(8,128)(2,1)S(1)} %shard_map.76), channel_id=1, replica_groups={{0,3,4,7,8,11,12,15,1,2,5,6,9,10,13,14},{16,19,20,23,24,27,28,31,17,18,..., dimensions={0} | all-to-all | bytes 1966080 | tf_op jit(solution)/shard_map/all_to_all | solution.py:274
  101.3 0.5 shard_map.77
  101.7 14.6 %all_to_all.16 = bf16[32,16,128]{2,1,0:T(8,128)(2,1)S(1)} all-to-all(bf16[32,16,128]{2,1,0:T(8,128)(2,1)S(1)} %bitcast.16), channel_id=1, replica_groups={{0,80,160,240,256,336,416,496,16,96,176,192,272,352,432,448,32,112,128,..., dimensions={0} | all-to-all | bytes 262144 | tf_op jit(solution)/shard_map/all_to_all | solution.py:276
  116.3 0.9 shard_map.78
  (1 shorter events, 0.0 us)
Async XLA Ops:
  2.2 26.0 %all-to-all-start = ((bf16[32,16,320]{2,1,0:T(8,128)(2,1)}), bf16[32,16,320]{2,1,0:T(8,128)(2,1)S(1)}, u32[]{:S(2)}, u32[]{:S(2)}) async-start(bf16[32,16,320]{2,1,0:T(8,128)(2,1)} %bitcast.6), calls=%async_computation | async-start | bytes 786432 | tf_op jit(solution)/shard_map/all_to_all | solution.py:266
  15.9 48.3 %collective-permute-start = (bf16[256,2560]{1,0:T(8,128)(2,1)}, bf16[256,2560]{1,0:T(8,128)(2,1)}, u32[]{:S(2)}, u32[]{:S(2)}) collective-permute-start(bf16[256,2560]{1,0:T(8,128)(2,1)} %bitcast.18), channel_id=1, source_target_pairs={{0,1},{1,0},{2,3},{3,2},{4,5},{5,4},{6,7},{7,6},{8,9},{9,8},{10,11... | collective-permute-start | bytes 3932168 | tf_op jit(solution)/shard_map/ppermute | solution.py:272
  18.8 46.9 %collective-permute-start.1 = (bf16[2560,256]{1,0:T(8,128)(2,1)}, bf16[2560,256]{1,0:T(8,128)(2,1)S(1)}, u32[]{:S(2)}, u32[]{:S(2)}) collective-permute-start(bf16[2560,256]{1,0:T(8,128)(2,1)} %bitcast.20), channel_id=1, source_target_pairs={{0,1},{1,0},{2,3},{3,2},{4,5},{5,4},{6,7},{7,6},{8,9},{9,8},{10,11... | collective-permute-start | bytes 3932168 | tf_op jit(solution)/shard_map/ppermute | solution.py:272
  20.7 45.0 %collective-permute-start.2 = (bf16[2560,256]{1,0:T(8,128)(2,1)}, bf16[2560,256]{1,0:T(8,128)(2,1)S(1)}, u32[]{:S(2)}, u32[]{:S(2)}) collective-permute-start(bf16[2560,256]{1,0:T(8,128)(2,1)} %bitcast.22), channel_id=1, source_target_pairs={{0,1},{1,0},{2,3},{3,2},{4,5},{5,4},{6,7},{7,6},{8,9},{9,8},{10,11... | collective-permute-start | bytes 3932168 | tf_op jit(solution)/shard_map/ppermute | solution.py:272
  64.2 1.7 %copy-start = (bf16[1,256,2560]{2,1,0:T(8,128)(2,1)S(1)}, bf16[1,256,2560]{2,1,0:T(8,128)(2,1)}, u32[]{:S(2)}) copy-start(bf16[1,256,2560]{2,1,0:T(8,128)(2,1)} %param.13) | copy-start | bytes 3932164
  64.2 2.1 %copy-start.1 = (bf16[1,2560,256]{2,1,0:T(8,128)(2,1)S(1)}, bf16[1,2560,256]{2,1,0:T(8,128)(2,1)}, u32[]{:S(2)}) copy-start(bf16[1,2560,256]{2,1,0:T(8,128)(2,1)} %param.11) | copy-start | bytes 3932164
  64.2 2.5 %copy-start.2 = (bf16[1,2560,256]{2,1,0:T(8,128)(2,1)S(1)}, bf16[1,2560,256]{2,1,0:T(8,128)(2,1)}, u32[]{:S(2)}) copy-start(bf16[1,2560,256]{2,1,0:T(8,128)(2,1)} %param.12) | copy-start | bytes 3932164

commit v7 on v6

--- a/solution.py
+++ b/solution.py
@@ -189,8 +189,9 @@
     rank = slot % ROWS
     heads = (row == slot).astype(BF)
     tails = (row == slot - rank + CAP + rank // 4).astype(BF)
-    out_ref[:128, :] = dot(recv_ref[...], heads, (0, 0)).astype(BF)
-    quarters = dot(recv_ref[...], tails, (0, 0))
+    both = dot(recv_ref[...], jnp.concatenate([heads, tails], axis=1), (0, 0))
+    out_ref[:128, :] = both[:, :TOK].astype(BF)
+    quarters = both[:, TOK:]
     last = quarters[:32]
     for i in range(1, 4):
         last = jnp.where(rank % 4 == i, quarters[32 * i : 32 * (i + 1)], last)

time: 118 us -> 118 us (level)
  no operation moved by 1% of the time
where the time goes in v7:
time: 118 us; the launch traced here: 117 us
  blocking collectives  80.1 us (68%)
  starting transfers between devices  20.9 us (18%)
  Pallas kernels  9.46 us (8%)
  waiting for transfers between devices  5.05 us (4%)
    all_gather x1, blocking collectives, body(): lax.all_gather(turned.astype(jnp.float16), 'etp', axis=0, tiled=True)  35 us
    all_to_all x1, blocking collectives, body(): lax.all_to_all(partial, 'etp', split_axis=0, concat_axis=0, tiled=True, a...  30.5 us
    all_to_all x1, blocking collectives, body(): lax.all_to_all(summed.reshape(EXPERTS, ROWS, 128), 'ep', split_axis=0, co...  14.6 us
    all_to_all x1, starting transfers between devices, body(): lax.all_to_all(send.reshape(EXPERTS, ROWS, 2 * WID), 'ep', split_axis=0,...  13.7 us
    ppermute x3, starting transfers between devices, body(): wg1, wu1, wd1 = (lax.ppermute(w, 'etp', other) for w in own)  7.2 us
    all_to_all x1, waiting for transfers between devices, body(): lax.all_to_all(send.reshape(EXPERTS, ROWS, 2 * WID), 'ep', split_axis=0,...  5.05 us
    pallas_call x1, Pallas kernels, expert_call(): call(expert_kernel, [SM] + [VM] * 10, shape((N_ETP, WID * 3 // 2, 128), B...  4.06 us
  transfers between devices with their start and end apart: 4, of which 1 were waited for; matrix products, arithmetic and copies ran while one was open for 0% of the time, Pallas kernels for 2%

profile of v7, /device:TPU:1, one launch (start us, length us, event | category | flops | bytes accessed | tf_op | source)
XLA Modules:
  0.0 117.2 jit_solution(15735692556944869739)
XLA Ops:
  0.0 2.2 %shard_map.73 = (bf16[512,320]{1,0:T(8,128)(2,1)}, s32[1,256]{1,0:T(1,128)S(1)}, f32[8,384]{1,0:T(8,128)S(1)}) custom-call(s32[1]{0:T(128)} %bitcast.me_ref, s32[1,256]{1,0:T(1,128)} %bitcast.28, bf16[160,256]{1,0:T(8,128)(2,1)} %bitcast.25, bf16[160,256]{1,0:T(8,128)(2,1)} %bitcast.26, bf16[32,160]{1,0:T(8,128)(2,1)} %bitcast.27), custom_call_target="tpu_custom_call" | custom-call | tf_op jit(solution)/shard_map/pallas_call | solution.py:254
  2.2 13.7 %all-to-all-start = ((bf16[32,16,320]{2,1,0:T(8,128)(2,1)}), bf16[32,16,320]{2,1,0:T(8,128)(2,1)S(1)}, u32[]{:S(2)}, u32[]{:S(2)}) async-start(bf16[32,16,320]{2,1,0:T(8,128)(2,1)} %bitcast.6), calls=%async_computation | async-start | bytes 786432 | tf_op jit(solution)/shard_map/all_to_all | solution.py:267
  15.9 2.9 %collective-permute-start = (bf16[256,2560]{1,0:T(8,128)(2,1)}, bf16[256,2560]{1,0:T(8,128)(2,1)}, u32[]{:S(2)}, u32[]{:S(2)}) collective-permute-start(bf16[256,2560]{1,0:T(8,128)(2,1)} %bitcast.18), channel_id=1, source_target_pairs={{0,1},{1,0},{2,3},{3,2},{4,5},{5,4},{6,7},{7,6},{8,9},{9,8},{10,11... | collective-permute-start | bytes 3932168 | tf_op jit(solution)/shard_map/ppermute | solution.py:273
  18.8 1.9 %collective-permute-start.1 = (bf16[2560,256]{1,0:T(8,128)(2,1)}, bf16[2560,256]{1,0:T(8,128)(2,1)S(1)}, u32[]{:S(2)}, u32[]{:S(2)}) collective-permute-start(bf16[2560,256]{1,0:T(8,128)(2,1)} %bitcast.20), channel_id=1, source_target_pairs={{0,1},{1,0},{2,3},{3,2},{4,5},{5,4},{6,7},{7,6},{8,9},{9,8},{10,11... | collective-permute-start | bytes 3932168 | tf_op jit(solution)/shard_map/ppermute | solution.py:273
  20.7 2.4 %collective-permute-start.2 = (bf16[2560,256]{1,0:T(8,128)(2,1)}, bf16[2560,256]{1,0:T(8,128)(2,1)S(1)}, u32[]{:S(2)}, u32[]{:S(2)}) collective-permute-start(bf16[2560,256]{1,0:T(8,128)(2,1)} %bitcast.22), channel_id=1, source_target_pairs={{0,1},{1,0},{2,3},{3,2},{4,5},{5,4},{6,7},{7,6},{8,9},{9,8},{10,11... | collective-permute-start | bytes 3932168 | tf_op jit(solution)/shard_map/ppermute | solution.py:273
  23.2 5.0 %all-to-all-done = bf16[32,16,320]{2,1,0:T(8,128)(2,1)S(1)} async-done(((bf16[32,16,320]{2,1,0:T(8,128)(2,1)}), bf16[32,16,320]{2,1,0:T(8,128)(2,1)S(1)}, u32[]{:S(2)}, u32[]{:S(2)}) %all-to-all-start) | async-done | bytes 327712 | tf_op jit(solution)/shard_map/all_to_all | solution.py:267
  28.2 0.4 shard_map.74
  28.7 35.0 %all-gather.1 = f16[5248,384]{1,0:T(8,128)(2,1)S(1)} all-gather(f16[328,384]{1,0:T(8,128)(2,1)S(1)} %convert_element_type.9), channel_id=1, replica_groups=mesh['ep'=32,'etp'=16] {'etp'}, dimensions={0}, use_global_device_ids=true | all-gather | bytes 4282368 | tf_op jit(solution)/shard_map/all_gather | solution.py:269
  63.7 0.5 slice_convert_fusion
  64.2 0.0 collective-permute-done.wd_ref
  64.2 0.0 copy-start
  64.2 0.0 copy-start.1
  64.2 0.0 copy-start.2
  64.2 1.5 %shard_map.75 = (bf16[256,2560]{1,0:T(8,128)(2,1)S(1)}, bf16[2560,256]{1,0:T(8,128)(2,1)S(1)}, f32[1,256]{1,0:T(1,128)S(1)}, f32[160,16]{1,0:T(8,128)S(1)}, bf16[256,2560]{1,0:T(8,128)(2,1)S(1)}) custom-call(bf16[16,328,128]{2,1,0:T(8,128)(2,1)S(1)} %get-tuple-element.22.lo_ref, bf16[16,328,128]{2,1,0:T(8,128)(2,1)S(1)} %get-tuple-element.21.hi_ref, ...), custom_call_target="tpu_custom_call" | custom-call | tf_op jit(solution)/shard_map/pallas_call | solution.py:224
  65.7 0.0 collective-permute-done.1.wg0
  65.7 0.0 collective-permute-done.2.wu0
  65.7 0.2 copy-done
  65.9 0.4 copy-done.1
  66.3 0.4 copy-done.2
  66.7 4.1 %shard_map.76 = bf16[16,240,128]{2,1,0:T(8,128)(2,1)S(1)} custom-call(s32[1]{0:T(128)} %bitcast.5.core_ref, bf16[256,2560]{1,0:T(8,128)(2,1)S(1)} %get-tuple-element.16.xt_ref, bf16[2560,256]{1,0:T(8,128)(2,1)S(1)} %get-tuple-element.17.g_ref, f32[1,256]{1,0:T(1,128)S(1)} %get-tuple-element.18.score_ref, f32[160,16]{1,0:T(8,128)S(1)} %get-tuple-element.19.router_ref, ...), custom_call_target="tpu_custom_call" | custom-call | flops 3355443200 | bytes 12582912 | tf_op jit(solution)/shard_map/pallas_call | solution.py:238
  70.8 30.5 %all_to_all.15.recv_ref = bf16[16,240,128]{2,1,0:T(8,128)(2,1)S(1)} all-to-all(bf16[16,240,128]{2,1,0:T(8,128)(2,1)S(1)} %shard_map.76), channel_id=1, replica_groups={{0,3,4,7,8,11,12,15,1,2,5,6,9,10,13,14},{16,19,20,23,24,27,28,31,17,18,..., dimensions={0} | all-to-all | bytes 1966080 | tf_op jit(solution)/shard_map/all_to_all | solution.py:275
  101.3 0.5 shard_map.77
  101.7 14.6 %all_to_all.16 = bf16[32,16,128]{2,1,0:T(8,128)(2,1)S(1)} all-to-all(bf16[32,16,128]{2,1,0:T(8,128)(2,1)S(1)} %bitcast.16), channel_id=1, replica_groups={{0,80,160,240,256,336,416,496,16,96,176,192,272,352,432,448,32,112,128,..., dimensions={0} | all-to-all | bytes 262144 | tf_op jit(solution)/shard_map/all_to_all | solution.py:277
  116.3 0.9 shard_map.78
  (1 shorter events, 0.0 us)
Async XLA Ops:
  2.2 26.0 %all-to-all-start = ((bf16[32,16,320]{2,1,0:T(8,128)(2,1)}), bf16[32,16,320]{2,1,0:T(8,128)(2,1)S(1)}, u32[]{:S(2)}, u32[]{:S(2)}) async-start(bf16[32,16,320]{2,1,0:T(8,128)(2,1)} %bitcast.6), calls=%async_computation | async-start | bytes 786432 | tf_op jit(solution)/shard_map/all_to_all | solution.py:267
  15.9 48.3 %collective-permute-start = (bf16[256,2560]{1,0:T(8,128)(2,1)}, bf16[256,2560]{1,0:T(8,128)(2,1)}, u32[]{:S(2)}, u32[]{:S(2)}) collective-permute-start(bf16[256,2560]{1,0:T(8,128)(2,1)} %bitcast.18), channel_id=1, source_target_pairs={{0,1},{1,0},{2,3},{3,2},{4,5},{5,4},{6,7},{7,6},{8,9},{9,8},{10,11... | collective-permute-start | bytes 3932168 | tf_op jit(solution)/shard_map/ppermute | solution.py:273
  18.8 46.9 %collective-permute-start.1 = (bf16[2560,256]{1,0:T(8,128)(2,1)}, bf16[2560,256]{1,0:T(8,128)(2,1)S(1)}, u32[]{:S(2)}, u32[]{:S(2)}) collective-permute-start(bf16[2560,256]{1,0:T(8,128)(2,1)} %bitcast.20), channel_id=1, source_target_pairs={{0,1},{1,0},{2,3},{3,2},{4,5},{5,4},{6,7},{7,6},{8,9},{9,8},{10,11... | collective-permute-start | bytes 3932168 | tf_op jit(solution)/shard_map/ppermute | solution.py:273
  20.7 45.0 %collective-permute-start.2 = (bf16[2560,256]{1,0:T(8,128)(2,1)}, bf16[2560,256]{1,0:T(8,128)(2,1)S(1)}, u32[]{:S(2)}, u32[]{:S(2)}) collective-permute-start(bf16[2560,256]{1,0:T(8,128)(2,1)} %bitcast.22), channel_id=1, source_target_pairs={{0,1},{1,0},{2,3},{3,2},{4,5},{5,4},{6,7},{7,6},{8,9},{9,8},{10,11... | collective-permute-start | bytes 3932168 | tf_op jit(solution)/shard_map/ppermute | solution.py:273
  64.2 1.7 %copy-start = (bf16[1,256,2560]{2,1,0:T(8,128)(2,1)S(1)}, bf16[1,256,2560]{2,1,0:T(8,128)(2,1)}, u32[]{:S(2)}) copy-start(bf16[1,256,2560]{2,1,0:T(8,128)(2,1)} %param.13) | copy-start | bytes 3932164
  64.2 2.1 %copy-start.1 = (bf16[1,2560,256]{2,1,0:T(8,128)(2,1)S(1)}, bf16[1,2560,256]{2,1,0:T(8,128)(2,1)}, u32[]{:S(2)}) copy-start(bf16[1,2560,256]{2,1,0:T(8,128)(2,1)} %param.11) | copy-start | bytes 3932164
  64.2 2.5 %copy-start.2 = (bf16[1,2560,256]{2,1,0:T(8,128)(2,1)S(1)}, bf16[1,2560,256]{2,1,0:T(8,128)(2,1)}, u32[]{:S(2)}) copy-start(bf16[1,2560,256]{2,1,0:T(8,128)(2,1)} %param.12) | copy-start | bytes 3932164
